TPU v7x, 32 devices: a whole 2x2x4 slice. The times are simulated.
32 devices in a mesh: rows: 8 (over y, x, core), grp: 4 (over z).
Axes of the slice: x: 2, y: 2, z: 4, core: 2. Of those that a mesh axis runs over, the one named last changes fastest.
Arguments:
- single: bfloat16 [768, 384], P('grp'), may hold values from -6 to 6
- pair: bfloat16 [768, 768, 128], P('rows', 'grp'), may hold values from -6 to 6
- chains: int32 [768], replicated, may hold values from 0 to 3, as said below
- noised: bfloat16 [8, 768, 768], P('rows', 'grp'), may hold values from -6 to 6
- w_gamma: bfloat16 [384, 768], replicated, may hold values from -0.3125 to 0.3125
- w_beta: bfloat16 [384, 768], replicated, may hold values from -0.3125 to 0.3125
- w_outgate: bfloat16 [384, 768], replicated, may hold values from -0.3125 to 0.3125
- w_query: bfloat16 [768, 768], replicated, may hold values from -0.21875 to 0.21875
- w_key: bfloat16 [768, 768], replicated, may hold values from -0.21875 to 0.21875
- w_value: bfloat16 [768, 768], replicated, may hold values from -0.21875 to 0.21875
- w_out: bfloat16 [768, 768], replicated, may hold values from -0.21875 to 0.21875
- w_pair: bfloat16 [128, 16], replicated, may hold values from -0.5 to 0.5
- chain_gain: float32 [16], replicated, may hold values from -3 to 6
- cotangent: bfloat16 [8, 768, 768], P('rows', 'grp'), may hold values from -6 to 6
Outputs:
- updated: bfloat16 [8, 768, 768], P('rows', 'grp')
- d_single: float32 [768, 384], P('grp')
- d_pair: bfloat16 [768, 768, 128], P('rows', 'grp')
Inputs may be any that keep to these rules, and one draw needn't show every extreme that they name: `chains`: chain numbers never fall along the tokens; each chain has 1 to 384 tokens, one exactly 384.
All inputs are finite; a program needn't handle non-finite values.
Results may differ from a plain program's by a relative error of at most 0.022.
Values may be sent and summed in bfloat16 or wider, within the bound.
No kernel may reach another device: no remote copies, remote signals or barrier semaphores. Data moves between devices by JAX's collectives and lax.ppermute only.
A program may use at most 128 MiB of HBM per device.

v0:
```python
import math

import jax
import jax.numpy as jnp
from jax import lax
from jax.sharding import PartitionSpec as P

EPSILON = 1e-05


def norm_rows(values):
    center = values - jnp.mean(values, axis=-1, keepdims=True)
    inverse = lax.rsqrt(jnp.mean(center * center, axis=-1, keepdims=True) + EPSILON)
    return (center * inverse, inverse)


def norm_back(grad_in, normed, inverse):
    grad_mean = jnp.mean(grad_in, axis=-1, keepdims=True)
    cross_mean = jnp.mean(grad_in * normed, axis=-1, keepdims=True)
    return inverse * (grad_in - grad_mean - normed * cross_mean)


def project(acts, weight):
    return jnp.einsum("std,de->ste", acts, weight, preferred_element_type=jnp.float32)


def project_back(acts, weight):
    return jnp.einsum("ste,de->std", acts, weight, preferred_element_type=jnp.float32)


def on_device(
    single,
    pair,
    chains,
    noised,
    w_gamma,
    w_beta,
    w_outgate,
    w_query,
    w_key,
    w_value,
    w_out,
    w_pair,
    chain_gain,
    cotangent,
):
    col_count = single.shape[0]
    row_count = pair.shape[0]
    head_count = w_pair.shape[1]
    model_width = w_query.shape[0]
    head_size = model_width // head_count
    sample_count = noised.shape[0]
    token_total = chains.shape[0]
    score_scale = 1.0 / math.sqrt(head_size)
    row_index = lax.axis_index("rows")
    group_index = lax.axis_index("grp")
    chain_rows = lax.dynamic_slice_in_dim(chains, row_index * row_count, row_count)
    chain_cols = lax.dynamic_slice_in_dim(chains, group_index * col_count, col_count)
    pair_norm, pair_inv = norm_rows(pair.astype(jnp.float32))
    projected = jnp.einsum(
        "ijc,ch->hij", pair_norm.astype(jnp.bfloat16), w_pair, preferred_element_type=jnp.float32
    )
    same_chain = (chain_rows[:, None] == chain_cols[None, :]).astype(jnp.float32)
    bias_block = (projected + chain_gain[:, None, None] * same_chain[None]).astype(jnp.bfloat16)
    bias_keys = lax.all_gather(bias_block, "rows", axis=1, tiled=True)
    single_norm, single_inv = norm_rows(single.astype(jnp.float32))
    single_b = single_norm.astype(jnp.bfloat16)
    cond_gamma = jax.nn.sigmoid(jnp.dot(single_b, w_gamma, preferred_element_type=jnp.float32))
    cond_beta = jnp.dot(single_b, w_beta, preferred_element_type=jnp.float32)
    out_gate = jax.nn.sigmoid(jnp.dot(single_b, w_outgate, preferred_element_type=jnp.float32))
    noised_f = noised.astype(jnp.float32)
    noised_norm, noised_inv = norm_rows(noised_f)
    x_b = (noised_norm * cond_gamma[None] + cond_beta[None]).astype(jnp.bfloat16)
    queries = project(x_b, w_query).astype(jnp.bfloat16)
    keys_own = project(x_b, w_key).astype(jnp.bfloat16)
    values_own = project(x_b, w_value).astype(jnp.bfloat16)
    queries_all = lax.all_gather(queries, "grp", axis=1, tiled=True)
    query_heads = queries_all.reshape(sample_count, token_total, head_count, head_size)
    key_heads = keys_own.reshape(sample_count, col_count, head_count, head_size)
    value_heads = values_own.reshape(sample_count, col_count, head_count, head_size)
    scores = (
        jnp.einsum("sihe,sjhe->shij", query_heads, key_heads, preferred_element_type=jnp.float32)
        * score_scale
        + bias_keys.astype(jnp.float32)[None]
    )
    exp_scores = jnp.exp(scores)
    exp_total = lax.psum(jnp.sum(exp_scores, axis=-1).astype(jnp.bfloat16), "grp").astype(
        jnp.float32
    )
    attn_prob = exp_scores / exp_total[..., None]
    prob_b = attn_prob.astype(jnp.bfloat16)
    attended_part = jnp.einsum(
        "shij,sjhe->sihe", prob_b, value_heads, preferred_element_type=jnp.float32
    )
    attended_part = attended_part.reshape(sample_count, token_total, model_width)
    attended = lax.psum_scatter(
        attended_part.astype(jnp.bfloat16), "grp", scatter_dimension=1, tiled=True
    )
    block_update = project(attended, w_out)
    updated = (noised_f + out_gate[None] * block_update).astype(jnp.bfloat16)
    grad_out = cotangent.astype(jnp.float32)
    gate_part = jnp.sum(grad_out * block_update, axis=0)
    grad_update = (grad_out * out_gate[None]).astype(jnp.bfloat16)
    grad_attn = project_back(grad_update, w_out).astype(jnp.bfloat16)
    grads_all = lax.all_gather(grad_attn, "grp", axis=1, tiled=True)
    grad_heads = grads_all.reshape(sample_count, token_total, head_count, head_size)
    grad_prob = jnp.einsum(
        "sihe,sjhe->shij", grad_heads, value_heads, preferred_element_type=jnp.float32
    )
    row_delta = lax.psum(
        jnp.sum(attn_prob * grad_prob, axis=-1).astype(jnp.bfloat16), "grp"
    ).astype(jnp.float32)
    grad_score = attn_prob * (grad_prob - row_delta[..., None])
    score_b = grad_score.astype(jnp.bfloat16)
    query_part = (
        jnp.einsum("shij,sjhe->sihe", score_b, key_heads, preferred_element_type=jnp.float32)
        * score_scale
    )
    query_part = query_part.reshape(sample_count, token_total, model_width)
    grad_query = lax.psum_scatter(
        query_part.astype(jnp.bfloat16), "grp", scatter_dimension=1, tiled=True
    )
    grad_key = (
        jnp.einsum("shij,sihe->sjhe", score_b, query_heads, preferred_element_type=jnp.float32)
        * score_scale
    )
    grad_value = jnp.einsum(
        "shij,sihe->sjhe", prob_b, grad_heads, preferred_element_type=jnp.float32
    )
    grad_key = grad_key.reshape(sample_count, col_count, model_width).astype(jnp.bfloat16)
    grad_value = grad_value.reshape(sample_count, col_count, model_width).astype(jnp.bfloat16)
    grad_input = (
        project_back(grad_query, w_query)
        + project_back(grad_key, w_key)
        + project_back(grad_value, w_value)
    )
    gamma_part = jnp.sum(grad_input * noised_norm, axis=0)
    beta_part = jnp.sum(grad_input, axis=0)
    gamma_sum, beta_sum, gate_sum = lax.psum((gamma_part, beta_part, gate_part), "rows")
    pre_gamma = (gamma_sum * cond_gamma * (1.0 - cond_gamma)).astype(jnp.bfloat16)
    pre_gate = (gate_sum * out_gate * (1.0 - out_gate)).astype(jnp.bfloat16)
    grad_snorm = jnp.dot(pre_gamma, w_gamma.T, preferred_element_type=jnp.float32)
    grad_snorm = grad_snorm + jnp.dot(
        beta_sum.astype(jnp.bfloat16), w_beta.T, preferred_element_type=jnp.float32
    )
    grad_snorm = grad_snorm + jnp.dot(pre_gate, w_outgate.T, preferred_element_type=jnp.float32)
    d_single = norm_back(grad_snorm, single_norm, single_inv)
    bias_part = jnp.sum(score_b, axis=0, dtype=jnp.float32)
    bias_own = lax.psum_scatter(bias_part, "rows", scatter_dimension=1, tiled=True)
    bias_grad = (bias_own * token_total).astype(jnp.bfloat16)
    grad_pairn = jnp.einsum("hij,ch->ijc", bias_grad, w_pair, preferred_element_type=jnp.float32)
    d_pair = norm_back(grad_pairn, pair_norm, pair_inv).astype(jnp.bfloat16)
    return (updated, d_single, d_pair)


def solution(mesh):
    in_specs = (
        P("grp", None),
        P("rows", "grp", None),
        P(),
        P("rows", "grp", None),
        P(),
        P(),
        P(),
        P(),
        P(),
        P(),
        P(),
        P(),
        P(),
        P("rows", "grp", None),
    )
    out_specs = (P("rows", "grp", None), P("grp", None), P("rows", "grp", None))
    return jax.shard_map(
        on_device, mesh=mesh, in_specs=in_specs, out_specs=out_specs, check_vma=False
    )
```

profile of v0, /device:TPU:0, one launch (start us, length us, event | category | flops | bytes accessed | tf_op | source)
XLA Modules:
  0.0 465.4 jit_solution(9771500407625404569)
XLA Ops:
  7.2 1.2 convert_reduce_fusion.1
  8.5 1.2 fusion.44
  9.7 1.1 convert_reduce_fusion.2
  10.8 1.1 fusion.60
  11.9 1.6 fusion.35
  13.5 2.2 convolution_convert_fusion
  15.8 0.4 fusion.32
  16.2 0.8 copy-done.7
  17.1 1.4 fusion.38
  18.5 2.4 convolution_convert_fusion.2
  21.0 0.8 dynamic_slice.6
  21.8 0.8 dynamic_slice.7
  22.7 4.3 convert_reduce_fusion
  27.0 7.7 %fusion.9 = f32[96,192]{1,0:T(8,128)S(1)} fusion(bf16[96,192,128]{2,1,0:T(8,128)(2,1)} %param.15, f32[96,192]{1,0:T(8,128)S(1)} %broadcast_multiply_fusion.2), kind=kLoop, calls=%fused_computation.11 | loop fusion | flops 9418752 | bytes 4866048 | tf_op jit(solution)/shard_map/reduce_sum | solution.py:13
  34.8 8.7 %fusion.20 = bf16[16,96,192]{2,0,1:T(8,128)(2,1)} fusion(bf16[96,192,128]{2,1,0:T(8,128)(2,1)S(1)} %bitcast.122, f32[96,192]{1,0:T(8,128)S(1)} %add_rsqrt_fusion, f32[96,192]{1,0:T(8,128)S(1)} %broadcast_multiply_fusion.2, f32[96,192]{1,0:T(8,128)S(1)} %compare_convert_fusion, f32[16]{0:T(128)S(1)} %copy-done.14, bf16[128,16]{0,1:T(8,128)(2,1)S(1)} %copy-done.12), kind=kOutput, calls=%fused_computation.26 | convolution fusion | flops 85819392 | bytes 5533760 | tf_op jit(solution)/shard_map/ijc,ch->hij/dot_general | solution.py:60
  43.6 1.7 convolution_convert_fusion.1
  45.2 0.9 copy.35
  46.2 1.7 convolution_convert_fusion.3
  47.8 0.9 copy.33
  48.8 0.2 all-gather.10.cloned.1.call-done
  49.0 2.4 copy.37
  51.3 29.4 %all-gather.8.cloned.1.call-done = bf16[768,768]{1,0:T(8,128)(2,1)} async-done(((bf16[192,768]{1,0:T(8,128)(2,1)}), bf16[768,768]{1,0:T(8,128)(2,1)}) %all-gather.8.cloned.1.call-update) | async-done | bytes 1179664 | tf_op jit(solution)/shard_map/all_gather | solution.py:77
  80.8 1.6 copy.34
  82.3 45.6 %all-gather.6.cloned.1.call-done = bf16[16,768,192]{2,0,1:T(8,128)(2,1)} async-done(((bf16[16,96,192]{2,0,1:T(8,128)(2,1)}), bf16[16,768,192]{2,0,1:T(8,128)(2,1)}) %all-gather.6.cloned.1.call-update) | async-done | bytes 4718608 | tf_op jit(solution)/shard_map/all_gather | solution.py:65
  127.9 8.6 %copy.36 = bf16[16,768,192]{1,2,0:T(8,128)(2,1)} copy(bf16[16,768,192]{2,0,1:T(8,128)(2,1)} %all-gather.6.cloned.1.call-done) | data formatting | bytes 9437184 | tf_op jit(solution)/shard_map/all_gather | solution.py:65
  136.5 6.6 %fusion.11 = (bf16[16,768]{1,0:T(8,128)(2,1)S(1)}, f32[16,768,192]{1,2,0:T(8,128)}) fusion(bf16[16,768,192]{1,2,0:T(8,128)(2,1)} %copy.36, bf16[768,16,48]{0,2,1:T(8,128)(2,1)S(1)} %bitcast.126, bf16[192,16,48]{0,2,1:T(8,128)(2,1)} %bitcast.137), kind=kOutput, calls=%fused_computation.16 | convolution fusion | flops 235917312 | bytes 15654912 | tf_op jit(solution)/shard_map/sihe,sjhe->shij/dot_general | solution.py:82
  143.1 18.9 %psum.35 = bf16[16,768]{1,0:T(8,128)(2,1)S(1)} all-reduce(bf16[16,768]{1,0:T(8,128)(2,1)S(1)} %get-tuple-element.14), channel_id=1, replica_groups=mesh['rows'=8,'grp'=4] {'grp'}, use_global_device_ids=true, to_apply=%region_7.0 | all-reduce | flops 12288 | bytes 49152 | tf_op jit(solution)/shard_map/psum | solution.py:87
  162.1 14.8 %multiply_reduce_fusion = (bf16[16,768]{1,0:T(8,128)(2,1)S(1)}, f32[16,768,192]{1,2,0:T(8,128)}, f32[16,768,192]{1,2,0:T(8,128)}) fusion(f32[16,768]{1,0:T(8,128)S(1)} %div.58, bf16[16,768,192]{1,2,0:T(8,128)(2,1)} %copy.36, f32[16,768,192]{1,2,0:T(8,128)} %get-tuple-element.15, bf16[768,16,48]{0,2,1:T(8,128)(2,1)} %bitcast.135, ...), kind=kOutput, calls=%fused_computation.13 | convolution fusion | flops 240635904 | bytes 34578432 | tf_op jit(solution)/shard_map/sihe,sjhe->shij/dot_general | solution.py:107
  176.9 16.6 %psum.36 = bf16[16,768]{1,0:T(8,128)(2,1)} all-reduce(bf16[16,768]{1,0:T(8,128)(2,1)S(1)} %get-tuple-element.9), channel_id=1, replica_groups=mesh['rows'=8,'grp'=4] {'grp'}, use_global_device_ids=true, to_apply=%region_10.0 | all-reduce | flops 12288 | bytes 49152 | tf_op jit(solution)/shard_map/psum | solution.py:110
  193.5 0.7 sub.72
  194.2 10.5 %multiply_convert_fusion = bf16[16,768,192]{1,2,0:T(8,128)(2,1)} fusion(f32[16,768,192]{1,2,0:T(8,128)} %get-tuple-element.10, f32[16,768,192]{1,2,0:T(8,128)} %get-tuple-element.16, f32[16,768]{1,0:T(8,128)S(1)} %sub.72), kind=kLoop, calls=%fused_computation.12 | loop fusion | flops 7077888 | bytes 23642112 | tf_op jit(solution)/shard_map/convert_element_type | solution.py:114
  204.7 4.4 multiply_convert_fusion.1
  209.1 6.7 %copy.41 = bf16[1,768,768]{2,0,1:T(2,128)(2,1)} copy(bf16[1,768,768]{1,2,0:T(8,128)(2,1)} %bitcast.133) | data formatting | bytes 2359296
  215.8 2.9 copy.49
  218.8 5.8 %fusion.21 = bf16[16,48,768]{2,1,0:T(8,128)(2,1)} fusion(bf16[192,16,48]{0,2,1:T(8,128)(2,1)} %bitcast.140, f32[16,768,192]{1,2,0:T(8,128)} %get-tuple-element.10), kind=kOutput, calls=%fused_computation.28 | convolution fusion | flops 229441536 | bytes 10911744 | tf_op jit(solution)/shard_map/shij,sjhe->sihe/dot_general | solution.py:92
  224.6 6.7 %copy.39 = bf16[1,768,768]{2,0,1:T(2,128)(2,1)} copy(bf16[1,768,768]{1,2,0:T(8,128)(2,1)} %bitcast.134) | data formatting | bytes 2359296
  231.3 2.9 copy.50
  234.3 4.8 %fusion.26 = bf16[16,48,192]{2,1,0:T(8,128)(2,1)} fusion(bf16[768,16,48]{0,2,1:T(8,128)(2,1)S(1)} %bitcast.127, bf16[16,768,192]{1,2,0:T(8,128)(2,1)} %multiply_convert_fusion), kind=kOutput, calls=%fused_computation.32 | convolution fusion | flops 226787328 | bytes 6193152 | tf_op jit(solution)/shard_map/shij,sihe->sjhe/dot_general | solution.py:124
  239.1 6.2 %fusion.27 = bf16[16,48,192]{2,1,0:T(8,128)(2,1)} fusion(bf16[768,16,48]{0,2,1:T(8,128)(2,1)S(1)} %bitcast.136, f32[16,768,192]{1,2,0:T(8,128)} %get-tuple-element.10), kind=kOutput, calls=%fused_computation.33 | convolution fusion | flops 228999168 | bytes 10911744 | tf_op jit(solution)/shard_map/shij,sihe->sjhe/dot_general | solution.py:127
  245.3 1.3 reduce-scatter.12.cloned.1.call-done
  246.5 2.1 reshape_bitcast_fusion
  248.6 2.0 copy.42
  250.6 1.7 fusion.48
  252.3 2.1 convolution_add_fusion.1
  254.4 0.6 convolution_add_fusion
  254.9 21.7 %reduce-scatter.10.cloned.1.call-done = bf16[192,768]{1,0:T(8,128)(2,1)} async-done(((bf16[768,768]{1,0:T(8,128)(2,1)}), bf16[192,768]{1,0:T(8,128)(2,1)}) %reduce-scatter.10.cloned.1.call-update) | async-done | bytes 294928
  276.6 1.3 reshape_bitcast_fusion.1
  277.9 1.2 copy.40
  279.1 2.7 fusion.46
  281.8 10.0 %copy.43 = f32[16,768,192]{2,0,1:T(8,128)} copy(bf16[16,768,192]{1,2,0:T(8,128)(2,1)} %multiply_convert_fusion) | data formatting | bytes 14155776
  291.8 13.2 %reshape.284 = f32[768,3072]{1,0:T(8,128)} reshape(f32[768,16,192]{2,1,0:T(8,128)} %bitcast.125) | data formatting | bytes 18874368
  305.1 31.0 %all-reduce.5 = bf16[192,768]{1,0:T(8,128)(2,1)S(1)} all-reduce(f32[192,768]{1,0:T(8,128)S(1)} %convolution_add_fusion), channel_id=1, replica_groups=mesh['rows'=8,'grp'=4] {'rows'}, use_global_device_ids=true, to_apply=%region_13.0 | all-reduce | flops 147456 | bytes 884736 | tf_op jit(solution)/shard_map/psum | solution.py:139
  336.1 2.6 all-reduce.4.cloned.1.call-done
  338.6 1.8 fusion.61
  340.4 0.4 convolution_add_fusion.3
  340.8 1.8 fusion.76
  342.6 0.9 fusion.59
  343.5 75.4 %reduce-scatter.14.cloned.1.call-done = f32[96,3072]{1,0:T(8,128)} async-done(((f32[768,3072]{1,0:T(8,128)}), f32[96,3072]{1,0:T(8,128)}) %reduce-scatter.14.cloned.1.call-update) | async-done | bytes 1179664
  418.9 2.9 reshape.285
  421.8 2.2 copy.44
  424.1 1.1 multiply_convert_fusion.2
  425.1 2.1 copy.38
  427.3 18.5 %fusion.75 = (f32[96,192]{1,0:T(8,128)S(1)}, f32[96,192]{1,0:T(8,128)S(1)}, f32[96,192,128]{2,1,0:T(8,128)S(1)}) fusion(f32[96,192]{1,0:T(8,128)S(1)} %copy-done.10, f32[96,192]{1,0:T(8,128)S(1)} %broadcast_multiply_fusion.2, bf16[96,192,128]{2,1,0:T(8,128)(2,1)} %param.15, bf16[16,96,192]{2,0,1:T(8,128)(2,1)S(1)} %copy.38, bf16[128,16]{0,1:T(8,128)(2,1)S(1)} %copy-done.13), kind=kOutput, calls=%fused_computation.108 | convolution fusion | flops 89616384 | bytes 15044608 | tf_op jit(solution)/shard_map/hij,ch->ijc/dot_general | solution.py:151
  445.9 12.7 %fusion.8 = bf16[96,192,128]{2,1,0:T(8,128)(2,1)} fusion(bf16[96,192,128]{2,1,0:T(8,128)(2,1)S(1)} %bitcast.124, f32[96,192,128]{2,1,0:T(8,128)S(1)} %get-tuple-element.18, f32[96,192]{1,0:T(8,128)S(1)} %broadcast_multiply_fusion, f32[96,192]{1,0:T(8,128)S(1)} %broadcast_multiply_fusion.1, f32[96,192]{1,0:T(8,128)S(1)} %copy-done.10, ...), kind=kLoop, calls=%fused_computation.10 | loop fusion | flops 18874368 | bytes 19169280 | tf_op jit(solution)/shard_map/convert_element_type | solution.py:152
  (64 shorter events, 0.7 us)
Async XLA Ops:
  7.2 6.3 %copy-start = (bf16[768,768]{1,0:T(8,128)(2,1)S(1)}, bf16[768,768]{1,0:T(8,128)(2,1)}, u32[]{:S(2)}) copy-start(bf16[768,768]{1,0:T(8,128)(2,1)} %param.24) | copy-start | bytes 3538948
  7.2 8.6 %copy-start.5 = (bf16[192,384]{1,0:T(8,128)(2,1)S(1)}, bf16[192,384]{1,0:T(8,128)(2,1)}, u32[]{:S(2)}) copy-start(bf16[192,384]{1,0:T(8,128)(2,1)} %param.14) | copy-start | bytes 442372
  7.2 8.6 %copy-start.11 = (bf16[384,768]{1,0:T(8,128)(2,1)S(1)}, bf16[384,768]{1,0:T(8,128)(2,1)}, u32[]{:S(2)}) copy-start(bf16[384,768]{1,0:T(8,128)(2,1)} %param.18) | copy-start | bytes 1769476
  7.2 41.8 %all-gather.10.cloned.1.call-start = ((), (), s32[]{:S(2)}) async-start(), calls=%async_computation.5 | async-start | bytes 1474560 | tf_op jit(solution)/shard_map/all_gather | solution.py:105
  9.7 7.4 %copy-start.2 = (bf16[1,192,768]{2,1,0:T(8,128)(2,1)S(1)}, bf16[1,192,768]{2,1,0:T(8,128)(2,1)}, u32[]{:S(2)}) copy-start(bf16[1,192,768]{2,1,0:T(8,128)(2,1)} %param.17) | copy-start | bytes 884740
  15.7 65.0 %all-gather.8.cloned.1.call-start = ((), (), s32[]{:S(2)}) async-start(), calls=%async_computation.4 | async-start | bytes 1474560 | tf_op jit(solution)/shard_map/all_gather | solution.py:77
  16.2 0.8 copy-start.7
  18.5 16.2 %slice-start = ((s8[4718592]{0:T(1024)(128)(4,1)}), s8[524288]{0:T(1024)(128)(4,1)S(1)}, s32[]{:S(2)}) async-start(s8[4718592]{0:T(1024)(128)(4,1)} %bitcast.121), calls=%async_computation.10 | async-start | bytes 1048576
  21.0 106.9 %all-gather.6.cloned.1.call-start = ((), (), s32[]{:S(2)}) async-start(), calls=%async_computation.3 | async-start | bytes 7077888 | tf_op jit(solution)/shard_map/all_gather | solution.py:65
  22.6 12.1 %slice-start.1 = ((s8[4718592]{0:T(1024)(128)(4,1)}), s8[4194304]{0:T(1024)(128)(4,1)S(1)}, s32[]{:S(2)}) async-start(s8[4718592]{0:T(1024)(128)(4,1)} %bitcast.121), calls=%async_computation.11 | async-start | bytes 8388608
  22.7 12.1 %copy-start.12 = (bf16[128,16]{0,1:T(8,128)(2,1)S(1)}, bf16[128,16]{0,1:T(8,128)(2,1)}, u32[]{:S(2)}) copy-start(bf16[128,16]{0,1:T(8,128)(2,1)} %param.25) | copy-start | bytes 12292
  22.7 12.1 %copy-start.14 = (f32[16]{0:T(128)S(1)}, f32[16]{0:T(128)}, u32[]{:S(2)}) copy-start(f32[16]{0:T(128)} %param.26) | copy-start | bytes 196
  34.8 8.7 %copy-start.9 = (f32[96,192]{1,0:T(8,128)}, f32[96,192]{1,0:T(8,128)S(1)}, u32[]{:S(2)}) copy-start(f32[96,192]{1,0:T(8,128)S(1)} %add_rsqrt_fusion) | copy-start | bytes 221188
  43.5 203.0 %reduce-scatter.12.cloned.1.call-start = ((), (), s32[]{:S(2)}) async-start(), calls=%async_computation.7 | async-start | bytes 1474560
  218.7 57.9 %reduce-scatter.10.cloned.1.call-start = ((), (), s32[]{:S(2)}) async-start(), calls=%async_computation.6 | async-start | bytes 1474560
  234.2 104.4 %all-reduce.4.cloned.1.call-start = ((), (), s32[]{:S(2)}) async-start(), calls=%async_computation.9 | async-start | bytes 2359296 | tf_op jit(solution)/shard_map/psum | solution.py:139
  234.3 4.8 %copy-start.4 = (bf16[768,768]{0,1:T(8,128)(2,1)S(1)}, bf16[768,768]{0,1:T(8,128)(2,1)}, u32[]{:S(2)}) copy-start(bf16[768,768]{0,1:T(8,128)(2,1)} %copy.37) | copy-start | bytes 3538948
  239.1 11.5 %copy-start.1 = (bf16[768,768]{1,0:T(8,128)(2,1)S(1)}, bf16[768,768]{1,0:T(8,128)(2,1)}, u32[]{:S(2)}) copy-start(bf16[768,768]{1,0:T(8,128)(2,1)} %param.21) | copy-start | bytes 3538948
  250.6 3.8 copy-start.3
  250.6 3.8 copy-start.8
  281.8 137.1 %reduce-scatter.14.cloned.1.call-start = ((), (), s32[]{:S(2)}) async-start(), calls=%async_computation.8 | async-start | bytes 10616832
  305.0 35.4 %copy-start.6 = (bf16[384,768]{1,0:T(8,128)(2,1)S(1)}, bf16[384,768]{1,0:T(8,128)(2,1)}, u32[]{:S(2)}) copy-start(bf16[384,768]{1,0:T(8,128)(2,1)} %param.19) | copy-start | bytes 1769476
  343.5 83.8 %copy-start.10 = (f32[96,192]{1,0:T(8,128)S(1)}, f32[96,192]{1,0:T(8,128)}, u32[]{:S(2)}) copy-start(f32[96,192]{1,0:T(8,128)} %copy-done.9) | copy-start | bytes 221188
  343.5 83.8 %copy-start.13 = (bf16[128,16]{0,1:T(8,128)(2,1)S(1)}, bf16[128,16]{0,1:T(8,128)(2,1)}, u32[]{:S(2)}) copy-start(bf16[128,16]{0,1:T(8,128)(2,1)} %param.25) | copy-start | bytes 12292
  424.0 21.9 %slice-start.2 = ((s8[4718592]{0:T(1024)(128)(4,1)}), s8[524288]{0:T(1024)(128)(4,1)S(1)}, s32[]{:S(2)}) async-start(s8[4718592]{0:T(1024)(128)(4,1)} %bitcast.123), calls=%async_computation.12 | async-start | bytes 1048576
  427.3 18.6 %slice-start.3 = ((s8[4718592]{0:T(1024)(128)(4,1)}), s8[4194304]{0:T(1024)(128)(4,1)S(1)}, s32[]{:S(2)}) async-start(s8[4718592]{0:T(1024)(128)(4,1)} %bitcast.123), calls=%async_computation.13 | async-start | bytes 8388608
Sparse Core Ops, SparseCore 0:
  15.8 33.0 all-gather.9
  51.1 29.6 all-gather.7
  83.2 44.6 all-gather.5
  218.9 27.6 reduce-scatter.11
  248.7 27.8 reduce-scatter.9
  281.9 56.6 all-reduce.3
  342.5 76.3 reduce-scatter.13
where the time goes:
time: 467 us; the launch traced here: 465 us
  waiting for transfers between devices  176 us (38%)
  matrix products  92.3 us (20%)
  local copies, waits for them, and re-layouts  73.1 us (16%)
  blocking collectives  66.5 us (14%)
  other arithmetic  42.5 us (9%)
  between operations  14.6 us (3%)
    unnamed x10, waiting for transfers between devices  98.5 us
    unnamed x50, local copies, waits for them, and re-layouts  55 us
    all_gather x1, waiting for transfers between devices, on_device(): bias_keys = lax.all_gather(bias_block, 'rows', axis=1, tiled=True)  45.6 us
    psum x1, blocking collectives, on_device(): lax.psum((gamma_part, beta_part, gate_part), 'rows')  31 us
    all_gather x1, waiting for transfers between devices, on_device(): queries_all = lax.all_gather(queries, 'grp', axis=1, tiled=True)  29.4 us
    psum x1, blocking collectives, on_device(): lax.psum(jnp.sum(exp_scores, axis=-1).astype(jnp.bfloat16), 'grp')  18.9 us
    dot_general x1, matrix products, on_device(): jnp.einsum('hij,ch->ijc', bias_grad, w_pair, preferred_element_type=jnp.f...  18.5 us
    psum x1, blocking collectives, on_device(): lax.psum(jnp.sum(attn_prob * grad_prob, axis=-1).astype(jnp.bfloat16), 'g...  16.6 us
  transfers between devices with their start and end apart: 7, of which 7 were waited for; matrix products, arithmetic and copies ran while one was open for 21% of the time, Pallas kernels for 0%

commit v1 on v0

--- a/solution.py
+++ b/solution.py
@@ -1,11 +1,17 @@
+import functools
 import math
 
 import jax
 import jax.numpy as jnp
 from jax import lax
+from jax.experimental import pallas as pl
+from jax.experimental.pallas import tpu as pltpu
 from jax.sharding import PartitionSpec as P
 
 EPSILON = 1e-05
+BF16 = jnp.bfloat16
+F32 = jnp.float32
+VMEM_LIMIT = 56 * 1024 * 1024
 
 
 def norm_rows(values):
@@ -20,15 +26,486 @@
     return inverse * (grad_in - grad_mean - normed * cross_mean)
 
 
+def mm(left, right):
+    return lax.dot_general(left, right, (((1,), (0,)), ((), ())), preferred_element_type=F32)
+
+
+def mm_nt(left, right):
+    return lax.dot_general(left, right, (((1,), (1,)), ((), ())), preferred_element_type=F32)
+
+
+def mm_tn(left, right):
+    return lax.dot_general(left, right, (((0,), (0,)), ((), ())), preferred_element_type=F32)
+
+
+def sigmoid(values):
+    return 1.0 / (1.0 + jnp.exp(-values))
+
+
+def params():
+    return pltpu.CompilerParams(vmem_limit_bytes=VMEM_LIMIT)
+
+
+def project_kernel(
+    single_ref,
+    noised_ref,
+    cot_ref,
+    w_gamma_ref,
+    w_beta_ref,
+    w_outgate_ref,
+    w_query_ref,
+    w_key_ref,
+    w_value_ref,
+    w_out_ref,
+    send_ref,
+    gamma_ref,
+    gate_ref,
+):
+    groups, _, width = send_ref.shape
+    part = width // 4
+    single_norm, _ = norm_rows(single_ref[...].astype(F32))
+    single_b = single_norm.astype(BF16)
+    cond_gamma = sigmoid(mm(single_b, w_gamma_ref[...]))
+    gamma_ref[...] = cond_gamma
+    out_gate = sigmoid(mm(single_b, w_outgate_ref[...]))
+    gate_ref[...] = out_gate
+    cond_beta = mm(single_b, w_beta_ref[...])
+    noised_norm, _ = norm_rows(noised_ref[...].astype(F32))
+    x_b = (noised_norm * cond_gamma + cond_beta).astype(BF16)
+
+    def put(slot, values):
+        rounded = values.astype(BF16)
+        for group in range(groups):
+            send_ref[group, :, slot * part : (slot + 1) * part] = rounded[
+                :, group * part : (group + 1) * part
+            ]
+
+    put(0, mm(x_b, w_query_ref[...]))
+    put(1, mm(x_b, w_key_ref[...]))
+    put(2, mm(x_b, w_value_ref[...]))
+    grad_update = (cot_ref[...].astype(F32) * out_gate).astype(BF16)
+    put(3, mm_nt(grad_update, w_out_ref[...]))
+
+
+def pair_norm(block, ones):
+    center = block.astype(F32) - mm(block, ones)
+    square = (center * center).astype(BF16)
+    inverse = lax.rsqrt(mm(square, ones) + EPSILON)
+    return center * inverse, inverse
+
+
+def lane_tiles(cols):
+    return [(tile, tile * 128, min(cols, tile * 128 + 128)) for tile in range(-(-cols // 128))]
+
+
+def bias_kernel(gain_ref, pair_ref, w_pair_ref, rows_ref, cols_ref, bias_ref, flat_ref):
+    _, step, cols, channels = pair_ref.shape
+    heads = gain_ref.shape[0]
+    groups, per_group = bias_ref.shape[:2]
+    ones = jnp.full((channels, channels), 1.0 / channels, BF16)
+    weight = w_pair_ref[...]
+    chain_cols = cols_ref[...]
+    for half in range(2):
+
+        def one_row(row, carry):
+            normed, _ = pair_norm(pair_ref[half, row], ones)
+            values = mm_nt(weight, normed.astype(BF16))
+            for tile, start, end in lane_tiles(cols):
+                piece = values[:, start:end]
+                if end - start < 128:
+                    blank = jnp.zeros((heads, 128 - end + start), F32)
+                    piece = jnp.concatenate([piece, blank], axis=1)
+                flat_ref[tile, pl.ds(row, heads, stride=step), :] = piece
+            return carry
+
+        lax.fori_loop(0, step, one_row, 0, unroll=4)
+        same = (rows_ref[half] == chain_cols).astype(F32)
+        for head in range(heads):
+            values = jnp.concatenate(
+                [
+                    flat_ref[tile, head * step : (head + 1) * step, : end - start]
+                    for tile, start, end in lane_tiles(cols)
+                ],
+                axis=1,
+            )
+            values = values + gain_ref[head] * same
+            bias_ref[head // per_group, head % per_group, :, half * cols : (half + 1) * cols] = (
+                values.astype(BF16)
+            )
+
+
+def pair_bias(pair, w_pair, chain_gain, chain_rows, chain_cols, groups):
+    rows, cols, channels = pair.shape
+    heads = w_pair.shape[1]
+    half = rows // 2
+    step = 16
+    return pl.pallas_call(
+        bias_kernel,
+        grid=(half // step,),
+        in_specs=[
+            pl.BlockSpec(memory_space=pltpu.SMEM),
+            pl.BlockSpec((2, step, cols, channels), lambda t: (0, t, 0, 0)),
+            pl.BlockSpec((heads, channels), lambda t: (0, 0)),
+            pl.BlockSpec((2, step, 1), lambda t: (0, t, 0)),
+            pl.BlockSpec((1, cols), lambda t: (0, 0)),
+        ],
+        out_specs=pl.BlockSpec(
+            (groups, heads // groups, step, 2 * cols), lambda t: (0, 0, t, 0)
+        ),
+        out_shape=jax.ShapeDtypeStruct((groups, heads // groups, half, 2 * cols), BF16),
+        scratch_shapes=[pltpu.VMEM((-(-cols // 128), heads * step, 128), F32)],
+        compiler_params=params(),
+    )(
+        chain_gain,
+        pair.reshape(2, half, cols, channels),
+        w_pair.T,
+        chain_rows.reshape(2, half, 1),
+        chain_cols.reshape(1, cols),
+    )
+
+
+def pair_back_kernel(pair_ref, grad_ref, w_pair_ref, out_ref, flat_ref, *, factor):
+    _, step, cols, channels = pair_ref.shape
+    groups, per_group = grad_ref.shape[:2]
+    heads = groups * per_group
+    ones = jnp.full((channels, channels), 1.0 / channels, BF16)
+    weight = w_pair_ref[...].astype(F32)
+    weight = weight - jnp.mean(weight, axis=-1, keepdims=True)
+    high = weight.astype(BF16)
+    low = (weight - high.astype(F32)).astype(BF16)
+    weights = jnp.concatenate([high, low], axis=0)
+    for half in range(2):
+        for head in range(heads):
+            values = grad_ref[
+                head // per_group, head % per_group, :, half * cols : (half + 1) * cols
+            ].astype(F32)
+            for tile, start, end in lane_tiles(cols):
+                flat_ref[tile, head * step : (head + 1) * step, : end - start] = values[
+                    :, start:end
+                ]
+
+        def one_row(row, carry):
+            normed, inverse = pair_norm(pair_ref[half, row], ones)
+            grads = jnp.concatenate(
+                [
+                    flat_ref[tile, pl.ds(row, heads, stride=step), :][:, : end - start]
+                    for tile, start, end in lane_tiles(cols)
+                ],
+                axis=1,
+            )
+            grads = jnp.concatenate([grads, grads], axis=0).astype(BF16)
+            grad_pair = mm_tn(grads, weights)
+            cross = mm((grad_pair * normed).astype(BF16), ones)
+            out_ref[half, row] = (
+                (factor * inverse) * (grad_pair - normed * cross)
+            ).astype(BF16)
+            return carry
+
+        lax.fori_loop(0, step, one_row, 0, unroll=4)
+
+
+def pair_back(pair, grad, w_pair, factor):
+    rows, cols, channels = pair.shape
+    groups, per_group = grad.shape[:2]
+    heads = groups * per_group
+    half = rows // 2
+    step = 16
+    out = pl.pallas_call(
+        functools.partial(pair_back_kernel, factor=factor),
+        grid=(half // step,),
+        in_specs=[
+            pl.BlockSpec((2, step, cols, channels), lambda t: (0, t, 0, 0)),
+            pl.BlockSpec((groups, per_group, step, 2 * cols), lambda t: (0, 0, t, 0)),
+            pl.BlockSpec((heads, channels), lambda t: (0, 0)),
+        ],
+        out_specs=pl.BlockSpec((2, step, cols, channels), lambda t: (0, t, 0, 0)),
+        out_shape=jax.ShapeDtypeStruct((2, half, cols, channels), BF16),
+        scratch_shapes=[pltpu.VMEM((-(-cols // 128), heads * step, 128), F32)],
+        compiler_params=params(),
+    )(pair.reshape(2, half, cols, channels), grad, w_pair.T)
+    return out.reshape(rows, cols, channels)
+
+
+def attention_kernel(
+    acts_ref,
+    bias_ref,
+    out_ref,
+    dbias_ref,
+    keys_t_ref,
+    values_t_ref,
+    query_t_ref,
+    grads_t_ref,
+    bias_full,
+    score_full,
+    att_sum,
+    gq_sum,
+    gk_sum,
+    gv_sum,
+    *,
+    head_size,
+    row_block,
+):
+    head = pl.program_id(0)
+    heads = pl.num_programs(0)
+    groups, cols, width = acts_ref.shape
+    tokens = groups * cols
+    part = width // 4
+    row_parts = bias_ref.shape[0]
+    half = bias_ref.shape[3]
+    scale = 1.0 / math.sqrt(head_size)
+    extra = att_sum.shape[1] - part
+
+    def piece(slot):
+        return acts_ref[:, :, slot * part : (slot + 1) * part].reshape(tokens, part)
+
+    @pl.when(head == 0)
+    def _():
+        query_t_ref[...] = piece(0).T
+        keys_t_ref[...] = piece(1).T
+        values_t_ref[...] = piece(2).T
+        grads_t_ref[...] = piece(3).T
+        att_sum[...] = jnp.zeros_like(att_sum)
+        gq_sum[...] = jnp.zeros_like(gq_sum)
+
+    for row_part in range(row_parts):
+        for group in range(groups):
+            for side in range(2):
+                top = row_part * 2 * half + side * half
+                bias_full[top : top + half, group * cols : (group + 1) * cols] = bias_ref[
+                    row_part, group, 0, :, side * cols : (side + 1) * cols
+                ]
+
+    lane = lax.broadcasted_iota(jnp.int32, (1, part), 1)
+    mine = (lane >= head * head_size) & (lane < (head + 1) * head_size)
+    zero = jnp.zeros((), BF16)
+    keys_m = jnp.where(mine, piece(1), zero)
+    values_m = jnp.concatenate(
+        [jnp.where(mine, piece(2), zero), jnp.ones((tokens, extra), BF16)], axis=1
+    )
+    feature = pl.multiple_of(head * head_size, head_size)
+    query_t = query_t_ref[pl.ds(feature, head_size), :]
+    grads_t = grads_t_ref[pl.ds(feature, head_size), :]
+    gk_t = jnp.zeros((head_size, tokens), F32)
+    gv_t = jnp.zeros((head_size, tokens), F32)
+    for top in range(0, tokens, row_block):
+        rows = slice(top, top + row_block)
+        query = jnp.where(mine, piece(0)[rows], zero)
+        grads = jnp.where(mine, piece(3)[rows], zero)
+        scores = mm(query, keys_t_ref[...]) * scale + bias_full[rows, :].astype(F32)
+        weights = jnp.exp(scores)
+        attended = mm(weights.astype(BF16), values_m)
+        inverse = 1.0 / attended[:, part : part + 1]
+        attended = attended[:, :part] * inverse
+        att_sum[rows, :part] += attended
+        delta = jnp.sum(attended * grads.astype(F32), axis=-1, keepdims=True)
+        prob = weights * inverse
+        grad_prob = mm(grads, values_t_ref[...])
+        score = (prob * (grad_prob - delta)).astype(BF16)
+        score_full[rows, :] = score
+        gq_sum[rows, :] += mm(score, keys_m)
+        gk_t = gk_t + mm(query_t[:, rows], score)
+        gv_t = gv_t + mm(grads_t[:, rows], prob.astype(BF16))
+    gk_sum[pl.ds(feature, head_size), :] = gk_t
+    gv_sum[pl.ds(feature, head_size), :] = gv_t
+
+    for row_part in range(row_parts):
+        for group in range(groups):
+            for side in range(2):
+                top = row_part * 2 * half + side * half
+                dbias_ref[row_part, group, 0, :, side * cols : (side + 1) * cols] = score_full[
+                    top : top + half, group * cols : (group + 1) * cols
+                ]
+
+    @pl.when(head == heads - 1)
+    def _():
+        results = (
+            gq_sum[...] * scale,
+            (gk_sum[...] * scale).T,
+            gv_sum[...].T,
+            att_sum[:, :part],
+        )
+        for slot, values in enumerate(results):
+            out_ref[:, :, slot * part : (slot + 1) * part] = values.astype(BF16).reshape(
+                groups, cols, part
+            )
+
+
+def attention(acts, bias, head_size):
+    groups, cols, width = acts.shape
+    tokens = groups * cols
+    part = width // 4
+    row_parts, _, heads, half, lanes = bias.shape
+    row_block = 256 if tokens % 256 == 0 else cols
+    spread = (row_parts, groups, 1, half, lanes)
+    padded = (part // 128 + 1) * 128
+    return pl.pallas_call(
+        functools.partial(attention_kernel, head_size=head_size, row_block=row_block),
+        grid=(heads,),
+        in_specs=[
+            pl.BlockSpec((groups, cols, width), lambda h: (0, 0, 0)),
+            pl.BlockSpec(spread, lambda h: (0, 0, h, 0, 0)),
+        ],
+        out_specs=[
+            pl.BlockSpec((groups, cols, width), lambda h: (0, 0, 0)),
+            pl.BlockSpec(spread, lambda h: (0, 0, h, 0, 0)),
+        ],
+        out_shape=[
+            jax.ShapeDtypeStruct((groups, cols, width), BF16),
+            jax.ShapeDtypeStruct(bias.shape, BF16),
+        ],
+        scratch_shapes=[
+            pltpu.VMEM((part, tokens), BF16),
+            pltpu.VMEM((part, tokens), BF16),
+            pltpu.VMEM((part, tokens), BF16),
+            pltpu.VMEM((part, tokens), BF16),
+            pltpu.VMEM((tokens, tokens), BF16),
+            pltpu.VMEM((tokens, tokens), BF16),
+            pltpu.VMEM((tokens, padded), F32),
+            pltpu.VMEM((tokens, part), F32),
+            pltpu.VMEM((part, tokens), F32),
+            pltpu.VMEM((part, tokens), F32),
+        ],
+        compiler_params=params(),
+    )(acts, bias)
+
+
+def finish_kernel(
+    got_ref,
+    single_ref,
+    noised_ref,
+    cot_ref,
+    gamma_ref,
+    gate_ref,
+    w_gamma_ref,
+    w_beta_ref,
+    w_outgate_ref,
+    w_query_ref,
+    w_key_ref,
+    w_value_ref,
+    w_out_ref,
+    updated_ref,
+    d_single_ref,
+):
+    groups, _, width = got_ref.shape
+    part = width // 4
+
+    def take(slot):
+        return jnp.concatenate(
+            [got_ref[group, :, slot * part : (slot + 1) * part] for group in range(groups)], axis=1
+        )
+
+    out_gate = gate_ref[...]
+    cond_gamma = gamma_ref[...]
+    block_update = mm(take(3), w_out_ref[...])
+    noised = noised_ref[...].astype(F32)
+    updated_ref[...] = (noised + out_gate * block_update).astype(BF16)
+    gate_part = cot_ref[...].astype(F32) * block_update
+    pre_gate = (gate_part * out_gate * (1.0 - out_gate)).astype(BF16)
+    grad_input = mm_nt(take(0), w_query_ref[...])
+    grad_input += mm_nt(take(1), w_key_ref[...])
+    grad_input += mm_nt(take(2), w_value_ref[...])
+    noised_norm, _ = norm_rows(noised)
+    pre_gamma = (grad_input * noised_norm * cond_gamma * (1.0 - cond_gamma)).astype(BF16)
+    grad_snorm = mm_nt(pre_gamma, w_gamma_ref[...])
+    grad_snorm += mm_nt(grad_input.astype(BF16), w_beta_ref[...])
+    grad_snorm += mm_nt(pre_gate, w_outgate_ref[...])
+    single_norm, single_inv = norm_rows(single_ref[...].astype(F32))
+    d_single_ref[...] = norm_back(grad_snorm, single_norm, single_inv)
+
+
+def split_heads(
+    single,
+    pair,
+    chains,
+    noised,
+    w_gamma,
+    w_beta,
+    w_outgate,
+    w_query,
+    w_key,
+    w_value,
+    w_out,
+    w_pair,
+    chain_gain,
+    cotangent,
+    *,
+    groups,
+):
+    cols, _ = single.shape
+    rows = pair.shape[0]
+    tokens = chains.shape[0]
+    width = noised.shape[2]
+    head_size = width // w_pair.shape[1]
+    row_index = lax.axis_index("rows")
+    group_index = lax.axis_index("grp")
+    chain_rows = lax.dynamic_slice_in_dim(chains, row_index * rows, rows)
+    chain_cols = lax.dynamic_slice_in_dim(chains, group_index * cols, cols)
+    bias_send = pair_bias(pair, w_pair, chain_gain, chain_rows, chain_cols, groups)
+    bias_own = lax.all_to_all(bias_send, "grp", 0, 0)
+    bias_all = lax.all_gather(bias_own, "rows", axis=0)
+    noised = noised[0]
+    cotangent = cotangent[0]
+    acts_send, cond_gamma, out_gate = pl.pallas_call(
+        project_kernel,
+        out_shape=[
+            jax.ShapeDtypeStruct((groups, cols, 4 * width // groups), BF16),
+            jax.ShapeDtypeStruct((cols, width), F32),
+            jax.ShapeDtypeStruct((cols, width), F32),
+        ],
+        compiler_params=params(),
+    )(
+        single,
+        noised,
+        cotangent,
+        w_gamma,
+        w_beta,
+        w_outgate,
+        w_query,
+        w_key,
+        w_value,
+        w_out,
+    )
+    acts = lax.all_to_all(acts_send, "grp", 0, 0)
+    grads_send, dbias = attention(acts, bias_all, head_size)
+    grads = lax.all_to_all(grads_send, "grp", 0, 0)
+    dbias_own = lax.psum_scatter(dbias, "rows", scatter_dimension=0, tiled=False)
+    dbias_back = lax.all_to_all(dbias_own, "grp", 0, 0)
+    updated, d_part = pl.pallas_call(
+        finish_kernel,
+        out_shape=[
+            jax.ShapeDtypeStruct((cols, width), BF16),
+            jax.ShapeDtypeStruct(single.shape, F32),
+        ],
+        compiler_params=params(),
+    )(
+        grads,
+        single,
+        noised,
+        cotangent,
+        cond_gamma,
+        out_gate,
+        w_gamma,
+        w_beta,
+        w_outgate,
+        w_query,
+        w_key,
+        w_value,
+        w_out,
+    )
+    d_single = lax.psum(d_part, "rows")
+    d_pair = pair_back(pair, dbias_back, w_pair, float(tokens))
+    return (updated[None], d_single, d_pair)
+
+
 def project(acts, weight):
-    return jnp.einsum("std,de->ste", acts, weight, preferred_element_type=jnp.float32)
+    return jnp.einsum("std,de->ste", acts, weight, preferred_element_type=F32)
 
 
 def project_back(acts, weight):
-    return jnp.einsum("ste,de->std", acts, weight, preferred_element_type=jnp.float32)
-
-
-def on_device(
+    return jnp.einsum("ste,de->std", acts, weight, preferred_element_type=F32)
+
+
+def split_keys(
     single,
     pair,
     chains,
@@ -171,6 +648,20 @@
         P("rows", "grp", None),
     )
     out_specs = (P("rows", "grp", None), P("grp", None), P("rows", "grp", None))
+    groups = mesh.shape["grp"]
+
+    def on_device(*args):
+        pair, noised, w_pair = args[1], args[3], args[11]
+        fits = (
+            pair.shape[0] % 32 == 0
+            and noised.shape[0] == 1
+            and noised.shape[1] % 64 == 0
+            and w_pair.shape[1] % groups == 0
+        )
+        if fits:
+            return split_heads(*args, groups=groups)
+        return split_keys(*args)
+
     return jax.shard_map(
         on_device, mesh=mesh, in_specs=in_specs, out_specs=out_specs, check_vma=False
     )

time: 467 us -> 238 us (0.51)
  waiting for transfers between devices: 176 us -> 48.3 us
  matrix products: 92.3 us -> 0 us
  Pallas kernels: 0 us -> 76.7 us
  local copies, waits for them, and re-layouts: 73.1 us -> 6.63 us
  other arithmetic: 42.5 us -> 0 us
  blocking collectives: 66.5 us -> 87.8 us
    unnamed x10 -> x3, waiting for transfers between devices: 98.5 us -> 0.05 us
    dot_general x22 -> x0, matrix products: 92.3 us -> none  [the longest x1 18.5 us: on_device(): jnp.einsum('hij,ch->ijc', bias_grad, w_pair, preferred_element_type=jnp.f...]
    all_to_all x0 -> x3, blocking collectives: none -> 87.8 us  [the longest x1 33.1 us: split_heads(): grads = lax.all_to_all(grads_send, 'grp', 0, 0)]
    pallas_call x0 -> x5, Pallas kernels: none -> 76.7 us  [the longest x1 24.1 us: pair_back(): pl.pallas_call(functools.partial(pair_back_kernel, factor=factor), grid=(...]
    all_gather x3 -> x1, waiting for transfers between devices: 75.2 us -> 0.01 us  [split_heads(): bias_all = lax.all_gather(bias_own, 'rows', axis=0)]
    psum x3 -> x0, blocking collectives: 66.5 us -> none  [the longest x1 31 us: on_device(): lax.psum((gamma_part, beta_part, gate_part), 'rows')]
    unnamed x50 -> x5, local copies, waits for them, and re-layouts: 55 us -> 3.75 us
    convert_element_type x4 -> x0, other arithmetic: 24.3 us -> none  [the longest x1 12.7 us: on_device(): d_pair = norm_back(grad_pairn, pair_norm, pair_inv).astype(jnp.bfloat16)]
  transfers between devices with their start and end apart: 7 -> 4, of which waited for: 7 -> 3; matrix products, arithmetic and copies ran while one was open for 21% -> 0% of each run, Pallas kernels for 0% -> 16%
where the time goes in v1:
time: 238 us
  blocking collectives  87.8 us (37%)
  Pallas kernels  76.7 us (32%)
  waiting for transfers between devices  48.3 us (20%)
  between operations  13.7 us (6%)
  local copies, waits for them, and re-layouts  6.63 us (3%)
  starting transfers between devices  4.67 us (2%)
    all_to_all x1, blocking collectives, split_heads(): grads = lax.all_to_all(grads_send, 'grp', 0, 0)  33.1 us
    all_to_all x1, blocking collectives, split_heads(): acts = lax.all_to_all(acts_send, 'grp', 0, 0)  32.4 us
    pallas_call x1, Pallas kernels, pair_back(): pl.pallas_call(functools.partial(pair_back_kernel, factor=factor), grid=(...  24.1 us
    pallas_call x1, Pallas kernels, pair_bias(): pl.pallas_call(bias_kernel, grid=(half // step,), in_specs=[pl.BlockSpec(...  23.7 us
    all_to_all x1, blocking collectives, split_heads(): bias_own = lax.all_to_all(bias_send, 'grp', 0, 0)  22.3 us
    psum x1, waiting for transfers between devices, split_heads(): d_single = lax.psum(d_part, 'rows')  20.6 us
    reduce_scatter x1, waiting for transfers between devices, split_heads(): lax.psum_scatter(dbias, 'rows', scatter_dimension=0, tiled=False)  19.3 us
    pallas_call x1, Pallas kernels, attention(): pl.pallas_call(functools.partial(attention_kernel, head_size=head_size, r...  15.3 us
  transfers between devices with their start and end apart: 4, of which 3 were waited for; matrix products, arithmetic and copies ran while one was open for 0% of the time, Pallas kernels for 16%

profile of v1, /device:TPU:0, one launch (start us, length us, event | category | flops | bytes accessed | tf_op | source)
XLA Modules:
  0.0 237.9 jit_solution(10386629347526019813)
XLA Ops:
  7.2 0.0 all-gather.3.cloned.1.call-start
  7.2 0.8 dynamic_slice.6
  8.0 1.3 dynamic_slice.7
  9.3 0.8 reshape.24.rows_ref
  10.1 23.7 %shard_map.158 = bf16[4,4,48,384]{3,2,1,0:T(8,128)(2,1)} custom-call(f32[16]{0:T(128)} %gain_ref.1, bf16[2,48,192,128]{3,2,1,0:T(8,128)(2,1)} %bitcast.9, bf16[16,128]{1,0:T(8,128)(2,1)} %bitcast.18, s32[2,48,1]{2,1,0:T(8,128)} %reshape.24.rows_ref, s32[1,192]{1,0:T(1,128)} %bitcast.20), custom_call_target="tpu_custom_call" | custom-call | tf_op jit(solution)/shard_map/pallas_call | solution.py:142
  33.8 22.3 %all_to_all.20 = bf16[4,4,48,384]{3,2,1,0:T(8,128)(2,1)} all-to-all(bf16[4,4,48,384]{3,2,1,0:T(8,128)(2,1)} %shard_map.158), channel_id=1, replica_groups=mesh['rows'=8,'grp'=4] {'grp'}, dimensions={0} | all-to-all | bytes 1179648 | tf_op jit(solution)/shard_map/all_to_all | solution.py:444
  56.1 0.0 all-gather.3.cloned.1.call-update
  56.1 0.0 reduce-scatter.2.cloned.1.call-start
  56.2 6.1 %shard_map.157 = (bf16[4,192,768]{2,1,0:T(8,128)(2,1)}, f32[192,768]{1,0:T(8,128)}, f32[192,768]{1,0:T(8,128)}) custom-call(bf16[192,384]{1,0:T(8,128)(2,1)} %single_ref.3, bf16[192,768]{1,0:T(8,128)(2,1)} %bitcast.13, bf16[192,768]{1,0:T(8,128)(2,1)} %bitcast.15, bf16[384,768]{1,0:T(8,128)(2,1)} %w_gamma_ref.3, bf16[384,768]{1,0:T(8,128)(2,1)} %w_beta_ref.3, ...), custom_call_target="tpu_custom_call" | custom-call | tf_op jit(solution)/shard_map/pallas_call | solution.py:448
  62.3 32.4 %all_to_all.21.acts_ref = bf16[4,192,768]{2,1,0:T(8,128)(2,1)} all-to-all(bf16[4,192,768]{2,1,0:T(8,128)(2,1)} %get-tuple-element.10), channel_id=1, replica_groups=mesh['rows'=8,'grp'=4] {'grp'}, dimensions={0} | all-to-all | bytes 2359296 | tf_op jit(solution)/shard_map/all_to_all | solution.py:468
  94.6 0.0 all-gather.3.cloned.1.call-done
  94.6 15.3 %shard_map.159 = (bf16[4,192,768]{2,1,0:T(8,128)(2,1)}, bf16[8,4,4,48,384]{4,3,2,1,0:T(8,128)(2,1)}) custom-call(bf16[4,192,768]{2,1,0:T(8,128)(2,1)} %all_to_all.21.acts_ref, bf16[8,4,4,48,384]{4,3,2,1,0:T(8,128)(2,1)} %bitcast.12), custom_call_target="tpu_custom_call" | custom-call | tf_op jit(solution)/shard_map/pallas_call | solution.py:341
  109.9 0.0 copy-start.1
  110.0 0.0 reduce-scatter.2.cloned.1.call-update
  110.0 1.2 copy-done.1
  111.2 33.1 %all_to_all.22.got_ref = bf16[4,192,768]{2,1,0:T(8,128)(2,1)} all-to-all(bf16[4,192,768]{2,1,0:T(8,128)(2,1)S(1)} %copy-done.1), channel_id=1, replica_groups=mesh['rows'=8,'grp'=4] {'grp'}, dimensions={0} | all-to-all | bytes 2359296 | tf_op jit(solution)/shard_map/all_to_all | solution.py:470
  144.3 19.3 %reduce-scatter.2.cloned.1.call-done = bf16[1,4,4,48,384]{4,3,2,1,0:T(8,128)(2,1)} async-done(((bf16[8,4,4,48,384]{4,3,2,1,0:T(8,128)(2,1)}), bf16[1,4,4,48,384]{4,3,2,1,0:T(8,128)(2,1)}) %reduce-scatter.2.cloned.1.call-update) | async-done | bytes 589840 | tf_op jit(solution)/shard_map/reduce_scatter | solution.py:471
  163.7 4.6 %all-to-all-start.3 = ((bf16[4,4,48,384]{3,2,1,0:T(8,128)(2,1)}), bf16[4,4,48,384]{3,2,1,0:T(8,128)(2,1)S(1)}, u32[]{:S(2)}, u32[]{:S(2)}) async-start(bf16[4,4,48,384]{3,2,1,0:T(8,128)(2,1)} %bitcast.17), calls=%async_computation.4 | async-start | bytes 1179648 | tf_op jit(solution)/shard_map/all_to_all | solution.py:472
  168.3 0.0 all-reduce.2.cloned.1.call-start
  168.3 7.5 %shard_map.160 = (bf16[192,768]{1,0:T(8,128)(2,1)}, f32[192,384]{1,0:T(8,128)}) custom-call(bf16[4,192,768]{2,1,0:T(8,128)(2,1)} %all_to_all.22.got_ref, bf16[192,384]{1,0:T(8,128)(2,1)} %single_ref.3, bf16[192,768]{1,0:T(8,128)(2,1)} %bitcast.14, bf16[192,768]{1,0:T(8,128)(2,1)} %bitcast.16, f32[192,768]{1,0:T(8,128)} %get-tuple-element.12.gamma_ref, ...), custom_call_target="tpu_custom_call" | custom-call | tf_op jit(solution)/shard_map/pallas_call | solution.py:473
  175.8 0.0 all-reduce.2.cloned.1.call-update
  175.8 8.3 %all-to-all-done.3.grad_ref = bf16[4,4,48,384]{3,2,1,0:T(8,128)(2,1)S(1)} async-done(((bf16[4,4,48,384]{3,2,1,0:T(8,128)(2,1)}), bf16[4,4,48,384]{3,2,1,0:T(8,128)(2,1)S(1)}, u32[]{:S(2)}, u32[]{:S(2)}) %all-to-all-start.3) | async-done | bytes 589856 | tf_op jit(solution)/shard_map/all_to_all | solution.py:472
  184.2 0.0 copy-start
  184.2 0.8 copy-done
  185.0 24.1 %shard_map.161 = bf16[2,48,192,128]{3,2,1,0:T(8,128)(2,1)} custom-call(bf16[2,48,192,128]{3,2,1,0:T(8,128)(2,1)} %bitcast.10, bf16[4,4,48,384]{3,2,1,0:T(8,128)(2,1)} %copy-done, bf16[16,128]{1,0:T(8,128)(2,1)} %bitcast.19), custom_call_target="tpu_custom_call" | custom-call | tf_op jit(solution)/shard_map/pallas_call | solution.py:213
  209.1 20.6 %all-reduce.2.cloned.1.call-done = f32[192,384]{1,0:T(8,128)} async-done(((f32[192,384]{1,0:T(8,128)}), f32[192,384]{1,0:T(8,128)}) %all-reduce.2.cloned.1.call-update) | async-done | bytes 294928 | tf_op jit(solution)/shard_map/psum | solution.py:495
  229.6 1.7 copy.20
Async XLA Ops:
  7.2 87.5 %all-gather.3.cloned.1.call-start = ((), (), s32[]{:S(2)}) async-start(), calls=%async_computation.7 | async-start | bytes 5308416 | tf_op jit(solution)/shard_map/all_gather | solution.py:445
  56.1 107.6 %reduce-scatter.2.cloned.1.call-start = ((), (), s32[]{:S(2)}) async-start(), calls=%async_computation.6 | async-start | bytes 5308416 | tf_op jit(solution)/shard_map/reduce_scatter | solution.py:471
  109.9 1.3 copy-start.1
  163.7 20.5 %all-to-all-start.3 = ((bf16[4,4,48,384]{3,2,1,0:T(8,128)(2,1)}), bf16[4,4,48,384]{3,2,1,0:T(8,128)(2,1)S(1)}, u32[]{:S(2)}, u32[]{:S(2)}) async-start(bf16[4,4,48,384]{3,2,1,0:T(8,128)(2,1)} %bitcast.17), calls=%async_computation.4 | async-start | bytes 1179648 | tf_op jit(solution)/shard_map/all_to_all | solution.py:472
  168.3 61.4 %all-reduce.2.cloned.1.call-start = ((), (), s32[]{:S(2)}) async-start(), calls=%async_computation.5 | async-start | bytes 589824 | tf_op jit(solution)/shard_map/psum | solution.py:495
  184.2 0.8 copy-start
Sparse Core Ops, SparseCore 0:
  56.2 38.0 all-gather.2
  110.1 53.5 reduce-scatter.1
  175.9 53.6 all-reduce.1

commit v2 on v1

--- a/solution.py
+++ b/solution.py
@@ -46,7 +46,16 @@
     return pltpu.CompilerParams(vmem_limit_bytes=VMEM_LIMIT)
 
 
+def smem():
+    return pl.BlockSpec(memory_space=pltpu.SMEM)
+
+
+def vmem():
+    return pl.BlockSpec(memory_space=pltpu.VMEM)
+
+
 def project_kernel(
+    group_ref,
     single_ref,
     noised_ref,
     cot_ref,
@@ -57,12 +66,14 @@
     w_key_ref,
     w_value_ref,
     w_out_ref,
-    send_ref,
-    gamma_ref,
-    gate_ref,
+    *rest,
+    groups,
 ):
-    groups, _, width = send_ref.shape
+    send_refs = rest[:groups]
+    gamma_ref, gate_ref, stage_ref = rest[groups:]
+    width = stage_ref.shape[2]
     part = width // 4
+    group_own = group_ref[0]
     single_norm, _ = norm_rows(single_ref[...].astype(F32))
     single_b = single_norm.astype(BF16)
     cond_gamma = sigmoid(mm(single_b, w_gamma_ref[...]))
@@ -73,10 +84,11 @@
     noised_norm, _ = norm_rows(noised_ref[...].astype(F32))
     x_b = (noised_norm * cond_gamma + cond_beta).astype(BF16)
 
-    def put(slot, values):
+    def put(kind, values):
         rounded = values.astype(BF16)
         for group in range(groups):
-            send_ref[group, :, slot * part : (slot + 1) * part] = rounded[
+            slot = lax.rem(group - group_own + groups, groups)
+            stage_ref[slot, :, kind * part : (kind + 1) * part] = rounded[
                 :, group * part : (group + 1) * part
             ]
 
@@ -85,202 +97,311 @@
     put(2, mm(x_b, w_value_ref[...]))
     grad_update = (cot_ref[...].astype(F32) * out_gate).astype(BF16)
     put(3, mm_nt(grad_update, w_out_ref[...]))
-
-
-def pair_norm(block, ones):
-    center = block.astype(F32) - mm(block, ones)
-    square = (center * center).astype(BF16)
-    inverse = lax.rsqrt(mm(square, ones) + EPSILON)
-    return center * inverse, inverse
+    for slot in range(groups):
+        send_refs[slot][...] = stage_ref[slot]
 
 
 def lane_tiles(cols):
     return [(tile, tile * 128, min(cols, tile * 128 + 128)) for tile in range(-(-cols // 128))]
 
 
-def bias_kernel(gain_ref, pair_ref, w_pair_ref, rows_ref, cols_ref, bias_ref, flat_ref):
+def mean_matrix(channels):
+    first = lax.broadcasted_iota(jnp.int32, (2 * channels, 2 * channels), 0) >= channels
+    second = lax.broadcasted_iota(jnp.int32, (2 * channels, 2 * channels), 1) >= channels
+    return jnp.where(first == second, 1.0 / channels, 0.0).astype(BF16)
+
+
+def center_rows(pair_ref, first, batch, means):
+    _, _, cols, channels = pair_ref.shape
+    both = jnp.concatenate(
+        [pair_ref[side, pl.ds(first, batch)].reshape(batch * cols, channels) for side in range(2)],
+        axis=1,
+    )
+    return both.astype(F32) - mm(both, means)
+
+
+def bias_kernel(
+    group_ref,
+    rows_ref,
+    chains_ref,
+    gain_ref,
+    pair_ref,
+    w_pair_ref,
+    cols_ref,
+    *rest,
+    groups,
+    batch,
+):
+    send_refs = rest[:groups]
+    stats_ref, flat_ref, gains_ref, stage_ref = rest[groups:]
     _, step, cols, channels = pair_ref.shape
     heads = gain_ref.shape[0]
-    groups, per_group = bias_ref.shape[:2]
-    ones = jnp.full((channels, channels), 1.0 / channels, BF16)
-    weight = w_pair_ref[...]
-    chain_cols = cols_ref[...]
-    for half in range(2):
-
-        def one_row(row, carry):
-            normed, _ = pair_norm(pair_ref[half, row], ones)
-            values = mm_nt(weight, normed.astype(BF16))
-            for tile, start, end in lane_tiles(cols):
-                piece = values[:, start:end]
-                if end - start < 128:
-                    blank = jnp.zeros((heads, 128 - end + start), F32)
-                    piece = jnp.concatenate([piece, blank], axis=1)
-                flat_ref[tile, pl.ds(row, heads, stride=step), :] = piece
-            return carry
-
-        lax.fori_loop(0, step, one_row, 0, unroll=4)
-        same = (rows_ref[half] == chain_cols).astype(F32)
-        for head in range(heads):
-            values = jnp.concatenate(
+    per_group = heads // groups
+    half = step * pl.num_programs(0)
+    group_own = group_ref[0]
+    row_base = rows_ref[0] * 2 * half + pl.program_id(0) * step
+    means = mean_matrix(channels)
+    weight = w_pair_ref[...].astype(F32).T.astype(BF16)
+    left = jnp.concatenate(
+        [
+            jnp.concatenate([weight, jnp.zeros((heads, channels), BF16)], axis=1),
+            jnp.concatenate(
                 [
-                    flat_ref[tile, head * step : (head + 1) * step, : end - start]
-                    for tile, start, end in lane_tiles(cols)
+                    jnp.zeros((heads, channels), BF16),
+                    jnp.full((heads, channels), 1.0 / channels, BF16),
                 ],
                 axis=1,
-            )
-            values = values + gain_ref[head] * same
-            bias_ref[head // per_group, head % per_group, :, half * cols : (half + 1) * cols] = (
-                values.astype(BF16)
-            )
-
-
-def pair_bias(pair, w_pair, chain_gain, chain_rows, chain_cols, groups):
+            ),
+        ],
+        axis=0,
+    )
+    chain_cols = cols_ref[pl.ds(group_own, 1), :]
+    for head in range(heads):
+        gains_ref[head : head + 1, :] = jnp.full((1, cols), gain_ref[head], F32)
+
+    def some_rows(index, carry):
+        first = index * batch
+        center = center_rows(pair_ref, first, batch, means)
+        center_b = center.astype(BF16)
+        square = (center * center).astype(BF16)
+        for inner in range(batch):
+            rows = slice(inner * cols, (inner + 1) * cols)
+            for side in range(2):
+                lanes = slice(side * channels, (side + 1) * channels)
+                right = jnp.concatenate([center_b[rows, lanes], square[rows, lanes]], axis=1)
+                sums = mm_nt(left, right)
+                inverse = lax.rsqrt(sums[heads : heads + 8] + EPSILON)
+                projected = sums[:heads] * inverse[:1]
+                stats_ref[side, first + inner, :heads, :] = projected
+                stats_ref[side, first + inner, heads:, :] = inverse
+                chain = chains_ref[row_base + side * half + first + inner]
+                same = (chain_cols == chain).astype(F32)
+                values = projected + gains_ref[...] * same
+                for tile, start, end in lane_tiles(cols):
+                    piece = values[:, start:end]
+                    if end - start < 128:
+                        blank = jnp.zeros((heads, 128 - end + start), F32)
+                        piece = jnp.concatenate([piece, blank], axis=1)
+                    flat_ref[side, tile, pl.ds(first + inner, heads, stride=step), :] = piece
+        return carry
+
+    lax.fori_loop(0, step // batch, some_rows, 0)
+    for head in range(heads):
+        slot = lax.rem(head // per_group - group_own + groups, groups)
+        values = jnp.concatenate(
+            [
+                flat_ref[side, tile, head * step : (head + 1) * step, : end - start]
+                for side in range(2)
+                for tile, start, end in lane_tiles(cols)
+            ],
+            axis=1,
+        )
+        stage_ref[slot, head % per_group] = values.astype(BF16)
+    for slot in range(groups):
+        send_refs[slot][...] = stage_ref[slot]
+
+
+def pair_bias(pair, w_pair, chain_gain, chains, group_index, row_index, groups):
     rows, cols, channels = pair.shape
     heads = w_pair.shape[1]
+    per_group = heads // groups
     half = rows // 2
     step = 16
-    return pl.pallas_call(
-        bias_kernel,
+    tiles = -(-cols // 128)
+    *sends, stats = pl.pallas_call(
+        functools.partial(bias_kernel, groups=groups, batch=4),
         grid=(half // step,),
         in_specs=[
-            pl.BlockSpec(memory_space=pltpu.SMEM),
+            smem(),
+            smem(),
+            smem(),
+            smem(),
             pl.BlockSpec((2, step, cols, channels), lambda t: (0, t, 0, 0)),
-            pl.BlockSpec((heads, channels), lambda t: (0, 0)),
-            pl.BlockSpec((2, step, 1), lambda t: (0, t, 0)),
-            pl.BlockSpec((1, cols), lambda t: (0, 0)),
+            pl.BlockSpec((channels, heads), lambda t: (0, 0)),
+            pl.BlockSpec((groups, cols), lambda t: (0, 0)),
         ],
-        out_specs=pl.BlockSpec(
-            (groups, heads // groups, step, 2 * cols), lambda t: (0, 0, t, 0)
-        ),
-        out_shape=jax.ShapeDtypeStruct((groups, heads // groups, half, 2 * cols), BF16),
-        scratch_shapes=[pltpu.VMEM((-(-cols // 128), heads * step, 128), F32)],
+        out_specs=[
+            pl.BlockSpec((per_group, step, 2 * cols), lambda t: (0, t, 0)) for _ in range(groups)
+        ]
+        + [pl.BlockSpec((2, step, heads + 8, cols), lambda t: (0, t, 0, 0))],
+        out_shape=[
+            jax.ShapeDtypeStruct((per_group, half, 2 * cols), BF16) for _ in range(groups)
+        ]
+        + [jax.ShapeDtypeStruct((2, half, heads + 8, cols), F32)],
+        scratch_shapes=[
+            pltpu.VMEM((2, tiles, heads * step, 128), F32),
+            pltpu.VMEM((heads, cols), F32),
+            pltpu.VMEM((groups, per_group, step, 2 * cols), BF16),
+        ],
         compiler_params=params(),
     )(
+        group_index,
+        row_index,
+        chains,
         chain_gain,
         pair.reshape(2, half, cols, channels),
-        w_pair.T,
-        chain_rows.reshape(2, half, 1),
-        chain_cols.reshape(1, cols),
-    )
-
-
-def pair_back_kernel(pair_ref, grad_ref, w_pair_ref, out_ref, flat_ref, *, factor):
+        w_pair,
+        chains.reshape(groups, cols),
+    )
+    return sends, stats
+
+
+def pair_back_kernel(group_ref, pair_ref, stats_ref, w_pair_ref, *rest, groups, factor, batch):
+    grad_refs = rest[:groups]
+    out_ref, flat_ref = rest[groups:]
     _, step, cols, channels = pair_ref.shape
-    groups, per_group = grad_ref.shape[:2]
+    per_group = grad_refs[0].shape[0]
     heads = groups * per_group
-    ones = jnp.full((channels, channels), 1.0 / channels, BF16)
-    weight = w_pair_ref[...].astype(F32)
+    group_own = group_ref[0]
+    means = mean_matrix(channels)
+    weight = w_pair_ref[...].astype(F32).T
     weight = weight - jnp.mean(weight, axis=-1, keepdims=True)
     high = weight.astype(BF16)
     low = (weight - high.astype(F32)).astype(BF16)
-    weights = jnp.concatenate([high, low], axis=0)
-    for half in range(2):
-        for head in range(heads):
-            values = grad_ref[
-                head // per_group, head % per_group, :, half * cols : (half + 1) * cols
-            ].astype(F32)
-            for tile, start, end in lane_tiles(cols):
-                flat_ref[tile, head * step : (head + 1) * step, : end - start] = values[
-                    :, start:end
-                ]
-
-        def one_row(row, carry):
-            normed, inverse = pair_norm(pair_ref[half, row], ones)
-            grads = jnp.concatenate(
-                [
-                    flat_ref[tile, pl.ds(row, heads, stride=step), :][:, : end - start]
-                    for tile, start, end in lane_tiles(cols)
-                ],
-                axis=1,
-            )
-            grads = jnp.concatenate([grads, grads], axis=0).astype(BF16)
-            grad_pair = mm_tn(grads, weights)
-            cross = mm((grad_pair * normed).astype(BF16), ones)
-            out_ref[half, row] = (
-                (factor * inverse) * (grad_pair - normed * cross)
-            ).astype(BF16)
-            return carry
-
-        lax.fori_loop(0, step, one_row, 0, unroll=4)
-
-
-def pair_back(pair, grad, w_pair, factor):
+    weights = jnp.concatenate([high, low, jnp.zeros((16, channels), BF16)], axis=0)
+    spread = lax.broadcasted_iota(jnp.int32, (2 * heads + 16, channels), 0)
+    spread = ((spread >= 2 * heads) & (spread < 2 * heads + 2)).astype(F32).astype(BF16)
+    weights = jnp.concatenate([weights, spread], axis=1)
+    blank = jnp.zeros((14, cols), F32)
+    for slot in range(groups):
+        source = lax.rem(group_own + slot, groups)
+        for head in range(per_group):
+            values = grad_refs[slot][head].astype(F32)
+            top = pl.multiple_of((source * per_group + head) * step, step)
+            for side in range(2):
+                for tile, start, end in lane_tiles(cols):
+                    flat_ref[side, tile, pl.ds(top, step), : end - start] = values[
+                        :, side * cols + start : side * cols + end
+                    ]
+
+    def some_rows(index, carry):
+        first = index * batch
+        center = center_rows(pair_ref, first, batch, means)
+        for side in range(2):
+            lefts = []
+            for inner in range(batch):
+                grads = jnp.concatenate(
+                    [
+                        flat_ref[side, tile, pl.ds(first + inner, heads, stride=step), :][
+                            :, : end - start
+                        ]
+                        for tile, start, end in lane_tiles(cols)
+                    ],
+                    axis=1,
+                )
+                projected = stats_ref[side, first + inner, :heads, :]
+                inverse = stats_ref[side, first + inner, heads : heads + 1, :]
+                cross = jnp.sum(grads * projected, axis=0, keepdims=True) * (1.0 / channels)
+                scaled = grads * (inverse * factor)
+                cross = cross * (inverse * inverse * factor)
+                cross_high = cross.astype(BF16).astype(F32)
+                lefts.append(
+                    jnp.concatenate(
+                        [scaled, scaled, cross_high, cross - cross_high, blank], axis=0
+                    )
+                )
+            for inner in range(batch):
+                rows = slice(inner * cols, (inner + 1) * cols)
+                lanes = slice(side * channels, (side + 1) * channels)
+                both = mm_tn(lefts[inner].astype(BF16), weights)
+                out_ref[side, first + inner] = (
+                    both[:, :channels] - center[rows, lanes] * both[:, channels:]
+                ).astype(BF16)
+        return carry
+
+    lax.fori_loop(0, step // batch, some_rows, 0)
+
+
+def pair_back(pair, stats, grads, w_pair, group_index, factor):
     rows, cols, channels = pair.shape
-    groups, per_group = grad.shape[:2]
+    groups = len(grads)
+    per_group = grads[0].shape[0]
     heads = groups * per_group
     half = rows // 2
     step = 16
+    tiles = -(-cols // 128)
     out = pl.pallas_call(
-        functools.partial(pair_back_kernel, factor=factor),
+        functools.partial(pair_back_kernel, groups=groups, factor=factor, batch=4),
         grid=(half // step,),
         in_specs=[
+            smem(),
             pl.BlockSpec((2, step, cols, channels), lambda t: (0, t, 0, 0)),
-            pl.BlockSpec((groups, per_group, step, 2 * cols), lambda t: (0, 0, t, 0)),
-            pl.BlockSpec((heads, channels), lambda t: (0, 0)),
-        ],
+            pl.BlockSpec((2, step, heads + 8, cols), lambda t: (0, t, 0, 0)),
+            pl.BlockSpec((channels, heads), lambda t: (0, 0)),
+        ]
+        + [pl.BlockSpec((per_group, step, 2 * cols), lambda t: (0, t, 0)) for _ in range(groups)],
         out_specs=pl.BlockSpec((2, step, cols, channels), lambda t: (0, t, 0, 0)),
         out_shape=jax.ShapeDtypeStruct((2, half, cols, channels), BF16),
-        scratch_shapes=[pltpu.VMEM((-(-cols // 128), heads * step, 128), F32)],
+        scratch_shapes=[pltpu.VMEM((2, tiles, heads * step, 128), F32)],
         compiler_params=params(),
-    )(pair.reshape(2, half, cols, channels), grad, w_pair.T)
+    )(group_index, pair.reshape(2, half, cols, channels), stats, w_pair, *grads)
     return out.reshape(rows, cols, channels)
 
 
-def attention_kernel(
-    acts_ref,
-    bias_ref,
-    out_ref,
-    dbias_ref,
-    keys_t_ref,
-    values_t_ref,
-    query_t_ref,
-    grads_t_ref,
-    bias_full,
-    score_full,
-    att_sum,
-    gq_sum,
-    gk_sum,
-    gv_sum,
-    *,
-    head_size,
-    row_block,
-):
+def attention_kernel(group_ref, bias_ref, *rest, groups, head_size, row_block):
+    acts_refs = rest[:groups]
+    out_refs = rest[groups : 2 * groups]
+    (
+        dbias_ref,
+        query_ref,
+        keys_ref,
+        values_ref,
+        grads_ref,
+        query_t_ref,
+        keys_t_ref,
+        values_t_ref,
+        grads_t_ref,
+        bias_full,
+        score_full,
+        att_sum,
+        gq_sum,
+        gk_sum,
+        gv_sum,
+    ) = rest[2 * groups :]
     head = pl.program_id(0)
     heads = pl.num_programs(0)
-    groups, cols, width = acts_ref.shape
+    group_own = group_ref[0]
+    cols, width = acts_refs[0].shape
     tokens = groups * cols
     part = width // 4
     row_parts = bias_ref.shape[0]
     half = bias_ref.shape[3]
     scale = 1.0 / math.sqrt(head_size)
     extra = att_sum.shape[1] - part
-
-    def piece(slot):
-        return acts_ref[:, :, slot * part : (slot + 1) * part].reshape(tokens, part)
+    plain = (query_ref, keys_ref, values_ref, grads_ref)
+    turned = (query_t_ref, keys_t_ref, values_t_ref, grads_t_ref)
 
     @pl.when(head == 0)
     def _():
-        query_t_ref[...] = piece(0).T
-        keys_t_ref[...] = piece(1).T
-        values_t_ref[...] = piece(2).T
-        grads_t_ref[...] = piece(3).T
+        for kind in range(4):
+            for slot in range(groups):
+                plain[kind][slot * cols : (slot + 1) * cols, :] = acts_refs[slot][
+                    :, kind * part : (kind + 1) * part
+                ]
+            turned[kind][...] = plain[kind][...].T
         att_sum[...] = jnp.zeros_like(att_sum)
         gq_sum[...] = jnp.zeros_like(gq_sum)
 
-    for row_part in range(row_parts):
-        for group in range(groups):
+    def places():
+        for row_part in range(row_parts):
+            owner, inside = divmod(row_part * 2 * half, cols)
+            slot = lax.rem(group_own - owner + groups, groups)
             for side in range(2):
-                top = row_part * 2 * half + side * half
-                bias_full[top : top + half, group * cols : (group + 1) * cols] = bias_ref[
-                    row_part, group, 0, :, side * cols : (side + 1) * cols
-                ]
+                top = pl.multiple_of(slot * cols + inside + side * half, 16)
+                for column in range(groups):
+                    yield row_part, column, side, pl.ds(top, half)
+
+    for row_part, column, side, rows in places():
+        bias_full[rows, column * cols : (column + 1) * cols] = bias_ref[
+            row_part, column, 0, :, side * cols : (side + 1) * cols
+        ]
 
     lane = lax.broadcasted_iota(jnp.int32, (1, part), 1)
     mine = (lane >= head * head_size) & (lane < (head + 1) * head_size)
     zero = jnp.zeros((), BF16)
-    keys_m = jnp.where(mine, piece(1), zero)
+    keys_m = jnp.where(mine, keys_ref[...], zero)
     values_m = jnp.concatenate(
-        [jnp.where(mine, piece(2), zero), jnp.ones((tokens, extra), BF16)], axis=1
+        [jnp.where(mine, values_ref[...], zero), jnp.ones((tokens, extra), BF16)], axis=1
     )
     feature = pl.multiple_of(head * head_size, head_size)
     query_t = query_t_ref[pl.ds(feature, head_size), :]
@@ -289,8 +410,8 @@
     gv_t = jnp.zeros((head_size, tokens), F32)
     for top in range(0, tokens, row_block):
         rows = slice(top, top + row_block)
-        query = jnp.where(mine, piece(0)[rows], zero)
-        grads = jnp.where(mine, piece(3)[rows], zero)
+        query = jnp.where(mine, query_ref[rows, :], zero)
+        grads = jnp.where(mine, grads_ref[rows, :], zero)
         scores = mm(query, keys_t_ref[...]) * scale + bias_full[rows, :].astype(F32)
         weights = jnp.exp(scores)
         attended = mm(weights.astype(BF16), values_m)
@@ -308,13 +429,10 @@
     gk_sum[pl.ds(feature, head_size), :] = gk_t
     gv_sum[pl.ds(feature, head_size), :] = gv_t
 
-    for row_part in range(row_parts):
-        for group in range(groups):
-            for side in range(2):
-                top = row_part * 2 * half + side * half
-                dbias_ref[row_part, group, 0, :, side * cols : (side + 1) * cols] = score_full[
-                    top : top + half, group * cols : (group + 1) * cols
-                ]
+    for row_part, column, side, rows in places():
+        dbias_ref[row_part, column, 0, :, side * cols : (side + 1) * cols] = score_full[
+            rows, column * cols : (column + 1) * cols
+        ]
 
     @pl.when(head == heads - 1)
     def _():
@@ -324,40 +442,36 @@
             gv_sum[...].T,
             att_sum[:, :part],
         )
-        for slot, values in enumerate(results):
-            out_ref[:, :, slot * part : (slot + 1) * part] = values.astype(BF16).reshape(
-                groups, cols, part
-            )
-
-
-def attention(acts, bias, head_size):
-    groups, cols, width = acts.shape
+        for kind, values in enumerate(results):
+            rounded = values.astype(BF16)
+            for slot in range(groups):
+                out_refs[slot][:, kind * part : (kind + 1) * part] = rounded[
+                    slot * cols : (slot + 1) * cols
+                ]
+
+
+def attention(group_index, acts, bias, head_size):
+    groups = len(acts)
+    cols, width = acts[0].shape
     tokens = groups * cols
     part = width // 4
     row_parts, _, heads, half, lanes = bias.shape
     row_block = 256 if tokens % 256 == 0 else cols
     spread = (row_parts, groups, 1, half, lanes)
     padded = (part // 128 + 1) * 128
-    return pl.pallas_call(
-        functools.partial(attention_kernel, head_size=head_size, row_block=row_block),
+    slots = [pl.BlockSpec((cols, width), lambda h: (0, 0)) for _ in range(groups)]
+    *grads, dbias = pl.pallas_call(
+        functools.partial(
+            attention_kernel, groups=groups, head_size=head_size, row_block=row_block
+        ),
         grid=(heads,),
-        in_specs=[
-            pl.BlockSpec((groups, cols, width), lambda h: (0, 0, 0)),
-            pl.BlockSpec(spread, lambda h: (0, 0, h, 0, 0)),
-        ],
-        out_specs=[
-            pl.BlockSpec((groups, cols, width), lambda h: (0, 0, 0)),
-            pl.BlockSpec(spread, lambda h: (0, 0, h, 0, 0)),
-        ],
-        out_shape=[
-            jax.ShapeDtypeStruct((groups, cols, width), BF16),
-            jax.ShapeDtypeStruct(bias.shape, BF16),
-        ],
-        scratch_shapes=[
-            pltpu.VMEM((part, tokens), BF16),
-            pltpu.VMEM((part, tokens), BF16),
-            pltpu.VMEM((part, tokens), BF16),
-            pltpu.VMEM((part, tokens), BF16),
+        in_specs=[smem(), pl.BlockSpec(spread, lambda h: (0, 0, h, 0, 0))] + slots,
+        out_specs=slots + [pl.BlockSpec(spread, lambda h: (0, 0, h, 0, 0))],
+        out_shape=[jax.ShapeDtypeStruct((cols, width), BF16) for _ in range(groups)]
+        + [jax.ShapeDtypeStruct(bias.shape, BF16)],
+        scratch_shapes=[pltpu.VMEM((tokens, part), BF16) for _ in range(4)]
+        + [pltpu.VMEM((part, tokens), BF16) for _ in range(4)]
+        + [
             pltpu.VMEM((tokens, tokens), BF16),
             pltpu.VMEM((tokens, tokens), BF16),
             pltpu.VMEM((tokens, padded), F32),
@@ -366,11 +480,12 @@
             pltpu.VMEM((part, tokens), F32),
         ],
         compiler_params=params(),
-    )(acts, bias)
+    )(group_index, bias, *acts)
+    return grads, dbias
 
 
 def finish_kernel(
-    got_ref,
+    group_ref,
     single_ref,
     noised_ref,
     cot_ref,
@@ -383,15 +498,20 @@
     w_key_ref,
     w_value_ref,
     w_out_ref,
-    updated_ref,
-    d_single_ref,
+    *rest,
+    groups,
 ):
-    groups, _, width = got_ref.shape
+    got_refs = rest[:groups]
+    updated_ref, d_single_ref, stage_ref = rest[groups:]
+    width = stage_ref.shape[2]
     part = width // 4
-
-    def take(slot):
+    for slot in range(groups):
+        stage_ref[lax.rem(group_ref[0] + slot, groups)] = got_refs[slot][...]
+
+    def take(kind):
         return jnp.concatenate(
-            [got_ref[group, :, slot * part : (slot + 1) * part] for group in range(groups)], axis=1
+            [stage_ref[group, :, kind * part : (kind + 1) * part] for group in range(groups)],
+            axis=1,
         )
 
     out_gate = gate_ref[...]
@@ -413,6 +533,25 @@
     d_single_ref[...] = norm_back(grad_snorm, single_norm, single_inv)
 
 
+def swap_groups(sends, direction):
+    groups = len(sends)
+    got = [sends[0]]
+    for shift in range(1, groups):
+        perm = [(index, (index + direction * shift) % groups) for index in range(groups)]
+        got.append(lax.ppermute(sends[shift], "grp", perm))
+    return got
+
+
+def sum_rows(values, row_total):
+    bit = 1
+    while bit < row_total:
+        perm = [(index, index ^ bit) for index in range(row_total)]
+        mine = values.astype(BF16)
+        values = mine.astype(F32) + lax.ppermute(mine, "rows", perm).astype(F32)
+        bit *= 2
+    return values
+
+
 def split_heads(
     single,
     pair,
@@ -430,30 +569,35 @@
     cotangent,
     *,
     groups,
+    row_total,
 ):
     cols, _ = single.shape
-    rows = pair.shape[0]
     tokens = chains.shape[0]
     width = noised.shape[2]
     head_size = width // w_pair.shape[1]
-    row_index = lax.axis_index("rows")
-    group_index = lax.axis_index("grp")
-    chain_rows = lax.dynamic_slice_in_dim(chains, row_index * rows, rows)
-    chain_cols = lax.dynamic_slice_in_dim(chains, group_index * cols, cols)
-    bias_send = pair_bias(pair, w_pair, chain_gain, chain_rows, chain_cols, groups)
-    bias_own = lax.all_to_all(bias_send, "grp", 0, 0)
+    row_index = lax.axis_index("rows").reshape(1)
+    group_index = lax.axis_index("grp").reshape(1)
+    bias_send, stats = pair_bias(
+        pair, w_pair, chain_gain, chains, group_index, row_index, groups
+    )
+    bias_own = jnp.stack(swap_groups(bias_send, 1))
     bias_all = lax.all_gather(bias_own, "rows", axis=0)
     noised = noised[0]
     cotangent = cotangent[0]
-    acts_send, cond_gamma, out_gate = pl.pallas_call(
-        project_kernel,
+    *acts_send, cond_gamma, out_gate = pl.pallas_call(
+        functools.partial(project_kernel, groups=groups),
+        in_specs=[smem()] + [vmem()] * 10,
         out_shape=[
-            jax.ShapeDtypeStruct((groups, cols, 4 * width // groups), BF16),
+            jax.ShapeDtypeStruct((cols, 4 * width // groups), BF16) for _ in range(groups)
+        ]
+        + [
             jax.ShapeDtypeStruct((cols, width), F32),
             jax.ShapeDtypeStruct((cols, width), F32),
         ],
+        scratch_shapes=[pltpu.VMEM((groups, cols, 4 * width // groups), BF16)],
         compiler_params=params(),
     )(
+        group_index,
         single,
         noised,
         cotangent,
@@ -465,20 +609,22 @@
         w_value,
         w_out,
     )
-    acts = lax.all_to_all(acts_send, "grp", 0, 0)
-    grads_send, dbias = attention(acts, bias_all, head_size)
-    grads = lax.all_to_all(grads_send, "grp", 0, 0)
+    acts = swap_groups(acts_send, 1)
+    grads_send, dbias = attention(group_index, acts, bias_all, head_size)
+    grads = swap_groups(grads_send, -1)
     dbias_own = lax.psum_scatter(dbias, "rows", scatter_dimension=0, tiled=False)
-    dbias_back = lax.all_to_all(dbias_own, "grp", 0, 0)
+    dbias_back = swap_groups([dbias_own[slot] for slot in range(groups)], -1)
     updated, d_part = pl.pallas_call(
-        finish_kernel,
+        functools.partial(finish_kernel, groups=groups),
+        in_specs=[smem()] + [vmem()] * (12 + groups),
         out_shape=[
             jax.ShapeDtypeStruct((cols, width), BF16),
             jax.ShapeDtypeStruct(single.shape, F32),
         ],
+        scratch_shapes=[pltpu.VMEM((groups, cols, 4 * width // groups), BF16)],
         compiler_params=params(),
     )(
-        grads,
+        group_index,
         single,
         noised,
         cotangent,
@@ -491,9 +637,10 @@
         w_key,
         w_value,
         w_out,
-    )
-    d_single = lax.psum(d_part, "rows")
-    d_pair = pair_back(pair, dbias_back, w_pair, float(tokens))
+        *grads,
+    )
+    d_single = sum_rows(d_part, row_total)
+    d_pair = pair_back(pair, stats, dbias_back, w_pair, group_index, float(tokens))
     return (updated[None], d_single, d_pair)
 
 
@@ -649,17 +796,20 @@
     )
     out_specs = (P("rows", "grp", None), P("grp", None), P("rows", "grp", None))
     groups = mesh.shape["grp"]
+    row_total = mesh.shape["rows"]
 
     def on_device(*args):
         pair, noised, w_pair = args[1], args[3], args[11]
         fits = (
             pair.shape[0] % 32 == 0
+            and pair.shape[1] % pair.shape[0] == 0
+            and row_total == 8
             and noised.shape[0] == 1
             and noised.shape[1] % 64 == 0
             and w_pair.shape[1] % groups == 0
         )
         if fits:
-            return split_heads(*args, groups=groups)
+            return split_heads(*args, groups=groups, row_total=row_total)
         return split_keys(*args)
 
     return jax.shard_map(

time: 238 us -> 185 us (0.78)
  blocking collectives: 87.8 us -> 0 us
  waiting for transfers between devices: 48.3 us -> 81.9 us
  Pallas kernels: 76.7 us -> 50.1 us
  starting transfers between devices: 4.67 us -> 25.8 us
  other arithmetic: 0 us -> 4.59 us
    all_to_all x3 -> x0, blocking collectives: 87.8 us -> none  [the longest x1 33.1 us: split_heads(): grads = lax.all_to_all(grads_send, 'grp', 0, 0)]
    ppermute x0 -> x15, waiting for transfers between devices: none -> 66.6 us  [the longest x12 58.7 us: swap_groups(): got.append(lax.ppermute(sends[shift], 'grp', perm))]
    pallas_call x5, Pallas kernels: 76.7 us -> 50.1 us  [the longest x1 16 us: attention(): pl.pallas_call(functools.partial(attention_kernel, groups=groups, head_si...]
    ppermute x0 -> x15, starting transfers between devices: none -> 25.7 us  [the longest x12 23 us: swap_groups(): got.append(lax.ppermute(sends[shift], 'grp', perm))]
    psum x1 -> x0, waiting for transfers between devices: 20.6 us -> none  [split_heads(): d_single = lax.psum(d_part, 'rows')]
    reduce_scatter x1, waiting for transfers between devices: 19.3 us -> 4.19 us  [split_heads(): lax.psum_scatter(dbias, 'rows', scatter_dimension=0, tiled=False)]
    all_gather x1, waiting for transfers between devices: 0.01 us -> 11 us  [split_heads(): bias_all = lax.all_gather(bias_own, 'rows', axis=0)]
    all_to_all x1 -> x0, waiting for transfers between devices: 8.34 us -> none  [split_heads(): dbias_back = lax.all_to_all(dbias_own, 'grp', 0, 0)]
  transfers between devices with their start and end apart: 4 -> 17, of which waited for: 3 -> 12; matrix products, arithmetic and copies ran while one was open for 0% -> 3% of each run, Pallas kernels for 16% -> 8%
where the time goes in v2:
time: 185 us; the launch traced here: 184 us
  waiting for transfers between devices  81.9 us (44%)
  Pallas kernels  50.1 us (27%)
  starting transfers between devices  25.8 us (14%)
  between operations  14.1 us (8%)
  local copies, waits for them, and re-layouts  7.07 us (4%)
  other arithmetic  4.59 us (2%)
    ppermute x12, waiting for transfers between devices, swap_groups(): got.append(lax.ppermute(sends[shift], 'grp', perm))  58.7 us
    ppermute x12, starting transfers between devices, swap_groups(): got.append(lax.ppermute(sends[shift], 'grp', perm))  23 us
    pallas_call x1, Pallas kernels, attention(): pl.pallas_call(functools.partial(attention_kernel, groups=groups, head_si...  16 us
    all_gather x1, waiting for transfers between devices, split_heads(): bias_all = lax.all_gather(bias_own, 'rows', axis=0)  11 us
    pallas_call x1, Pallas kernels, pair_bias(): pl.pallas_call(functools.partial(bias_kernel, groups=groups, batch=4), gr...  10.4 us
    pallas_call x1, Pallas kernels, pair_back(): pl.pallas_call(functools.partial(pair_back_kernel, groups=groups, factor=...  9.63 us
    ppermute x3, waiting for transfers between devices, sum_rows(): values = mine.astype(F32) + lax.ppermute(mine, 'rows', perm).astype(F32)  7.96 us
    pallas_call x1, Pallas kernels, split_heads(): pl.pallas_call(functools.partial(finish_kernel, groups=groups), in_specs=...  7.62 us
  transfers between devices with their start and end apart: 17, of which 12 were waited for; matrix products, arithmetic and copies ran while one was open for 3% of the time, Pallas kernels for 8%

profile of v2, /device:TPU:0, one launch (start us, length us, event | category | flops | bytes accessed | tf_op | source)
XLA Modules:
  0.0 183.6 jit_solution(11687218965959556272)
XLA Ops:
  7.2 0.0 all-gather.3.cloned.1.call-start
  7.2 1.3 reshape.33.cols_ref
  8.6 1.4 copy.19.w_pair_ref
  9.9 10.4 %shard_map.158 = (bf16[4,48,384]{2,1,0:T(8,128)(2,1)}, bf16[4,48,384]{2,1,0:T(8,128)(2,1)}, bf16[4,48,384]{2,1,0:T(8,128)(2,1)}, bf16[4,48,384]{2,1,0:T(8,128)(2,1)}, f32[2,48,24,192]{3,2,1,0:T(8,128)}) custom-call(s32[1]{0:T(128)} %bitcast.group_ref, s32[1]{0:T(128)} %bitcast.3.rows_ref, s32[768]{0:T(1024)} %chains_ref.1, f32[16]{0:T(128)} %gain_ref.1, ...), custom_call_target="tpu_custom_call" | custom-call | tf_op jit(solution)/shard_map/pallas_call | solution.py:211
  20.3 3.0 %collective-permute-start = (bf16[4,48,384]{2,1,0:T(8,128)(2,1)}, bf16[4,48,384]{2,1,0:T(8,128)(2,1)S(1)}, u32[]{:S(2)}, u32[]{:S(2)}) collective-permute-start(bf16[4,48,384]{2,1,0:T(8,128)(2,1)} %get-tuple-element.24), channel_id=1, source_target_pairs={{0,1},{1,2},{2,3},{3,0},{4,5},{5,6},{6,7},{7,4},{8,9},{9,10},{10,1... | collective-permute-start | bytes 442376 | tf_op jit(solution)/shard_map/ppermute | solution.py:541
  23.3 2.6 %collective-permute-start.1 = (bf16[4,48,384]{2,1,0:T(8,128)(2,1)}, bf16[4,48,384]{2,1,0:T(8,128)(2,1)S(1)}, u32[]{:S(2)}, u32[]{:S(2)}) collective-permute-start(bf16[4,48,384]{2,1,0:T(8,128)(2,1)} %get-tuple-element.25), channel_id=1, source_target_pairs={{0,2},{1,3},{2,0},{3,1},{4,6},{5,7},{6,4},{7,5},{8,10},{9,11},{10,... | collective-permute-start | bytes 442376 | tf_op jit(solution)/shard_map/ppermute | solution.py:541
  25.9 1.3 collective-permute-start.2
  27.3 3.1 %collective-permute-done = bf16[4,48,384]{2,1,0:T(8,128)(2,1)S(1)} collective-permute-done((bf16[4,48,384]{2,1,0:T(8,128)(2,1)}, bf16[4,48,384]{2,1,0:T(8,128)(2,1)S(1)}, u32[]{:S(2)}, u32[]{:S(2)}) %collective-permute-start) | collective-permute-done | bytes 147488 | tf_op jit(solution)/shard_map/ppermute | solution.py:541
  30.3 5.5 %collective-permute-done.1 = bf16[4,48,384]{2,1,0:T(8,128)(2,1)S(1)} collective-permute-done((bf16[4,48,384]{2,1,0:T(8,128)(2,1)}, bf16[4,48,384]{2,1,0:T(8,128)(2,1)S(1)}, u32[]{:S(2)}, u32[]{:S(2)}) %collective-permute-start.1) | collective-permute-done | bytes 147488 | tf_op jit(solution)/shard_map/ppermute | solution.py:541
  35.8 0.0 collective-permute-done.2
  35.8 1.8 pad_maximum_fusion
  37.7 0.0 all-gather.3.cloned.1.call-update
  37.7 0.0 reduce-scatter.2.cloned.1.call-start
  37.7 6.5 %shard_map.157 = (bf16[192,768]{1,0:T(8,128)(2,1)}, bf16[192,768]{1,0:T(8,128)(2,1)}, bf16[192,768]{1,0:T(8,128)(2,1)}, bf16[192,768]{1,0:T(8,128)(2,1)}, f32[192,768]{1,0:T(8,128)}, /*index=5*/f32[192,768]{1,0:T(8,128)}) custom-call(s32[1]{0:T(128)} %bitcast.group_ref, bf16[192,384]{1,0:T(8,128)(2,1)} %single_ref.3, bf16[192,768]{1,0:T(8,128)(2,1)} %bitcast.24, ...), custom_call_target="tpu_custom_call" | custom-call | tf_op jit(solution)/shard_map/pallas_call | solution.py:587
  44.3 3.6 %collective-permute-start.3 = (bf16[192,768]{1,0:T(8,128)(2,1)}, bf16[192,768]{1,0:T(8,128)(2,1)S(1)}, u32[]{:S(2)}, u32[]{:S(2)}) collective-permute-start(bf16[192,768]{1,0:T(8,128)(2,1)} %get-tuple-element.28), channel_id=1, source_target_pairs={{0,1},{1,2},{2,3},{3,0},{4,5},{5,6},{6,7},{7,4},{8,9},{9,10},{10,1... | collective-permute-start | bytes 884744 | tf_op jit(solution)/shard_map/ppermute | solution.py:541
  47.9 1.6 collective-permute-start.4
  49.5 0.8 collective-permute-start.5
  50.3 6.9 %collective-permute-done.3.rest_1_ = bf16[192,768]{1,0:T(8,128)(2,1)S(1)} collective-permute-done((bf16[192,768]{1,0:T(8,128)(2,1)}, bf16[192,768]{1,0:T(8,128)(2,1)S(1)}, u32[]{:S(2)}, u32[]{:S(2)}) %collective-permute-start.3) | collective-permute-done | bytes 294944 | tf_op jit(solution)/shard_map/ppermute | solution.py:541
  57.2 0.0 copy-start
  57.2 10.8 %collective-permute-done.4.rest_2_ = bf16[192,768]{1,0:T(8,128)(2,1)S(1)} collective-permute-done((bf16[192,768]{1,0:T(8,128)(2,1)}, bf16[192,768]{1,0:T(8,128)(2,1)S(1)}, u32[]{:S(2)}, u32[]{:S(2)}) %collective-permute-start.4) | collective-permute-done | bytes 294944 | tf_op jit(solution)/shard_map/ppermute | solution.py:541
  68.1 0.0 copy-start.1
  68.1 0.0 collective-permute-done.5.rest_3_
  68.1 0.0 copy-start.3
  68.1 11.0 %all-gather.3.cloned.1.call-done = bf16[32,4,48,384]{3,2,1,0:T(8,128)(2,1)} async-done(((bf16[4,4,48,384]{3,2,1,0:T(8,128)(2,1)}), bf16[32,4,48,384]{3,2,1,0:T(8,128)(2,1)}) %all-gather.3.cloned.1.call-update) | async-done | bytes 4718608 | tf_op jit(solution)/shard_map/all_gather | solution.py:584
  79.1 0.0 copy-done
  79.1 0.0 copy-done.1
  79.1 0.0 copy-done.3
  79.1 16.0 %shard_map.159 = (bf16[192,768]{1,0:T(8,128)(2,1)}, bf16[192,768]{1,0:T(8,128)(2,1)}, bf16[192,768]{1,0:T(8,128)(2,1)}, bf16[192,768]{1,0:T(8,128)(2,1)}, bf16[8,4,4,48,384]{4,3,2,1,0:T(8,128)(2,1)}) custom-call(s32[1]{0:T(128)} %bitcast.group_ref, bf16[8,4,4,48,384]{4,3,2,1,0:T(8,128)(2,1)} %bitcast.22, bf16[192,768]{1,0:T(8,128)(2,1)} %get-tuple-element.27.rest_0_, ...), custom_call_target="tpu_custom_call" | custom-call | tf_op jit(solution)/shard_map/pallas_call | solution.py:463
  95.1 0.0 copy-start.9
  95.1 0.0 reduce-scatter.2.cloned.1.call-update
  95.1 0.9 copy-done.11
  96.1 3.3 %collective-permute-start.6 = (bf16[192,768]{1,0:T(8,128)(2,1)S(1)}, bf16[192,768]{1,0:T(8,128)(2,1)S(1)}, u32[]{:S(2)}, u32[]{:S(2)}) collective-permute-start(bf16[192,768]{1,0:T(8,128)(2,1)S(1)} %copy-done.11), channel_id=1, source_target_pairs={{0,3},{1,0},{2,1},{3,2},{4,7},{5,4},{6,5},{7,6},{8,11},{9,8},{10,9... | collective-permute-start | bytes 884744 | tf_op jit(solution)/shard_map/ppermute | solution.py:541
  99.4 0.0 copy-done.10
  99.4 0.0 collective-permute-start.7
  99.4 0.0 copy-done.9
  99.4 1.1 collective-permute-start.8
  100.5 6.3 %collective-permute-done.6.rest_1_ = bf16[192,768]{1,0:T(8,128)(2,1)S(1)} collective-permute-done((bf16[192,768]{1,0:T(8,128)(2,1)S(1)}, bf16[192,768]{1,0:T(8,128)(2,1)S(1)}, u32[]{:S(2)}, u32[]{:S(2)}) %collective-permute-start.6) | collective-permute-done | bytes 294944 | tf_op jit(solution)/shard_map/ppermute | solution.py:541
  106.8 18.3 %collective-permute-done.7.rest_2_ = bf16[192,768]{1,0:T(8,128)(2,1)S(1)} collective-permute-done((bf16[192,768]{1,0:T(8,128)(2,1)S(1)}, bf16[192,768]{1,0:T(8,128)(2,1)S(1)}, u32[]{:S(2)}, u32[]{:S(2)}) %collective-permute-start.7) | collective-permute-done | bytes 294944 | tf_op jit(solution)/shard_map/ppermute | solution.py:541
  125.1 0.0 collective-permute-done.8.rest_3_
  125.1 0.0 copy-done.2
  125.1 0.7 copy-done.4
  125.8 0.1 copy-done.5
  126.0 7.6 %shard_map.160 = (bf16[192,768]{1,0:T(8,128)(2,1)}, f32[192,384]{1,0:T(8,128)}) custom-call(s32[1]{0:T(128)} %bitcast.group_ref, bf16[192,384]{1,0:T(8,128)(2,1)} %single_ref.3, bf16[192,768]{1,0:T(8,128)(2,1)} %bitcast.25, bf16[192,768]{1,0:T(8,128)(2,1)} %bitcast.27, f32[192,768]{1,0:T(8,128)} %get-tuple-element.21.gamma_ref, ...), custom_call_target="tpu_custom_call" | custom-call | tf_op jit(solution)/shard_map/pallas_call | solution.py:617
  133.6 1.0 convert_element_type.27
  134.6 0.1 collective-permute-start.9
  134.7 1.4 collective-permute-done.9
  136.0 1.0 add_convert_fusion.1
  137.0 1.5 collective-permute-start.10
  138.6 6.6 %collective-permute-done.10 = bf16[192,384]{1,0:T(8,128)(2,1)S(1)} collective-permute-done((bf16[192,384]{1,0:T(8,128)(2,1)S(1)}, bf16[192,384]{1,0:T(8,128)(2,1)S(1)}, u32[]{:S(2)}, u32[]{:S(2)}) %collective-permute-start.10) | collective-permute-done | bytes 147488 | tf_op jit(solution)/shard_map/ppermute | solution.py:550
  145.2 1.1 collective-permute-start.11
  146.3 4.2 %reduce-scatter.2.cloned.1.call-done = bf16[1,4,4,48,384]{4,3,2,1,0:T(8,128)(2,1)} async-done(((bf16[8,4,4,48,384]{4,3,2,1,0:T(8,128)(2,1)}), bf16[1,4,4,48,384]{4,3,2,1,0:T(8,128)(2,1)}) %reduce-scatter.2.cloned.1.call-update) | async-done | bytes 589840 | tf_op jit(solution)/shard_map/reduce_scatter | solution.py:615
  150.5 1.8 %slice_bitcast_fusion = (bf16[4,48,384]{2,1,0:T(8,128)(2,1)S(1)}, bf16[4,48,384]{2,1,0:T(8,128)(2,1)S(1)}, bf16[4,48,384]{2,1,0:T(8,128)(2,1)S(1)}, bf16[4,48,384]{2,1,0:T(8,128)(2,1)}) fusion(bf16[1,4,4,48,384]{4,3,2,1,0:T(8,128)(2,1)} %reduce-scatter.2.cloned.1.call-done), kind=kLoop, calls=%fused_computation.4 | loop fusion | bytes 1179648 | tf_op jit(solution)/shard_map/squeeze | solution.py:616
  152.4 2.7 %collective-permute-start.14 = (bf16[4,48,384]{2,1,0:T(8,128)(2,1)S(1)}, bf16[4,48,384]{2,1,0:T(8,128)(2,1)S(1)}, u32[]{:S(2)}, u32[]{:S(2)}) collective-permute-start(bf16[4,48,384]{2,1,0:T(8,128)(2,1)S(1)} %get-tuple-element.39), channel_id=1, source_target_pairs={{0,1},{1,2},{2,3},{3,0},{4,5},{5,6},{6,7},{7,4},{8,9},{9,10},{10,1... | collective-permute-start | bytes 442376 | tf_op jit(solution)/shard_map/ppermute | solution.py:541
  155.1 1.0 collective-permute-start.13
  156.1 1.8 collective-permute-start.12
  157.9 0.0 collective-permute-done.11
  157.9 0.7 convert_add_fusion
  158.6 2.3 %collective-permute-done.14.rest_3_ = bf16[4,48,384]{2,1,0:T(8,128)(2,1)S(1)} collective-permute-done((bf16[4,48,384]{2,1,0:T(8,128)(2,1)S(1)}, bf16[4,48,384]{2,1,0:T(8,128)(2,1)S(1)}, u32[]{:S(2)}, u32[]{:S(2)}) %collective-permute-start.14) | collective-permute-done | bytes 147488 | tf_op jit(solution)/shard_map/ppermute | solution.py:541
  161.0 5.4 %collective-permute-done.13.rest_2_ = bf16[4,48,384]{2,1,0:T(8,128)(2,1)S(1)} collective-permute-done((bf16[4,48,384]{2,1,0:T(8,128)(2,1)S(1)}, bf16[4,48,384]{2,1,0:T(8,128)(2,1)S(1)}, u32[]{:S(2)}, u32[]{:S(2)}) %collective-permute-start.13) | collective-permute-done | bytes 147488 | tf_op jit(solution)/shard_map/ppermute | solution.py:541
  166.4 0.0 collective-permute-done.12.rest_1_
  166.4 0.0 copy-done.6
  166.4 0.6 copy-done.7
  167.0 0.1 copy-done.8
  167.1 9.6 %shard_map.161 = bf16[2,48,192,128]{3,2,1,0:T(8,128)(2,1)} custom-call(s32[1]{0:T(128)} %bitcast.group_ref, bf16[2,48,192,128]{3,2,1,0:T(8,128)(2,1)} %bitcast.21, f32[2,48,24,192]{3,2,1,0:T(8,128)} %get-tuple-element.37.stats_ref, bf16[128,16]{1,0:T(8,128)(2,1)} %copy.19.w_pair_ref, bf16[4,48,384]{2,1,0:T(8,128)(2,1)} %get-tuple-element.42.rest_0_, ...), custom_call_target="tpu_custom_call" | custom-call | tf_op jit(solution)/shard_map/pallas_call | solution.py:323
  (9 shorter events, 0.1 us)
Async XLA Ops:
  7.2 71.9 %all-gather.3.cloned.1.call-start = ((), (), s32[]{:S(2)}) async-start(), calls=%async_computation.2 | async-start | bytes 5308416 | tf_op jit(solution)/shard_map/all_gather | solution.py:584
  20.3 10.0 %collective-permute-start = (bf16[4,48,384]{2,1,0:T(8,128)(2,1)}, bf16[4,48,384]{2,1,0:T(8,128)(2,1)S(1)}, u32[]{:S(2)}, u32[]{:S(2)}) collective-permute-start(bf16[4,48,384]{2,1,0:T(8,128)(2,1)} %get-tuple-element.24), channel_id=1, source_target_pairs={{0,1},{1,2},{2,3},{3,0},{4,5},{5,6},{6,7},{7,4},{8,9},{9,10},{10,1... | collective-permute-start | bytes 442376 | tf_op jit(solution)/shard_map/ppermute | solution.py:541
  23.3 12.5 %collective-permute-start.1 = (bf16[4,48,384]{2,1,0:T(8,128)(2,1)}, bf16[4,48,384]{2,1,0:T(8,128)(2,1)S(1)}, u32[]{:S(2)}, u32[]{:S(2)}) collective-permute-start(bf16[4,48,384]{2,1,0:T(8,128)(2,1)} %get-tuple-element.25), channel_id=1, source_target_pairs={{0,2},{1,3},{2,0},{3,1},{4,6},{5,7},{6,4},{7,5},{8,10},{9,11},{10,... | collective-permute-start | bytes 442376 | tf_op jit(solution)/shard_map/ppermute | solution.py:541
  25.9 9.9 %collective-permute-start.2 = (bf16[4,48,384]{2,1,0:T(8,128)(2,1)}, bf16[4,48,384]{2,1,0:T(8,128)(2,1)S(1)}, u32[]{:S(2)}, u32[]{:S(2)}) collective-permute-start(bf16[4,48,384]{2,1,0:T(8,128)(2,1)} %get-tuple-element.26), channel_id=1, source_target_pairs={{0,3},{1,0},{2,1},{3,2},{4,7},{5,4},{6,5},{7,6},{8,11},{9,8},{10,9... | collective-permute-start | bytes 442376 | tf_op jit(solution)/shard_map/ppermute | solution.py:541
  37.7 112.8 %reduce-scatter.2.cloned.1.call-start = ((), (), s32[]{:S(2)}) async-start(), calls=%async_computation.1 | async-start | bytes 5308416 | tf_op jit(solution)/shard_map/reduce_scatter | solution.py:615
  44.3 13.0 %collective-permute-start.3 = (bf16[192,768]{1,0:T(8,128)(2,1)}, bf16[192,768]{1,0:T(8,128)(2,1)S(1)}, u32[]{:S(2)}, u32[]{:S(2)}) collective-permute-start(bf16[192,768]{1,0:T(8,128)(2,1)} %get-tuple-element.28), channel_id=1, source_target_pairs={{0,1},{1,2},{2,3},{3,0},{4,5},{5,6},{6,7},{7,4},{8,9},{9,10},{10,1... | collective-permute-start | bytes 884744 | tf_op jit(solution)/shard_map/ppermute | solution.py:541
  47.9 20.2 %collective-permute-start.4 = (bf16[192,768]{1,0:T(8,128)(2,1)}, bf16[192,768]{1,0:T(8,128)(2,1)S(1)}, u32[]{:S(2)}, u32[]{:S(2)}) collective-permute-start(bf16[192,768]{1,0:T(8,128)(2,1)} %get-tuple-element.29), channel_id=1, source_target_pairs={{0,2},{1,3},{2,0},{3,1},{4,6},{5,7},{6,4},{7,5},{8,10},{9,11},{10,... | collective-permute-start | bytes 884744 | tf_op jit(solution)/shard_map/ppermute | solution.py:541
  49.5 18.6 %collective-permute-start.5 = (bf16[192,768]{1,0:T(8,128)(2,1)}, bf16[192,768]{1,0:T(8,128)(2,1)S(1)}, u32[]{:S(2)}, u32[]{:S(2)}) collective-permute-start(bf16[192,768]{1,0:T(8,128)(2,1)} %get-tuple-element.30), channel_id=1, source_target_pairs={{0,3},{1,0},{2,1},{3,2},{4,7},{5,4},{6,5},{7,6},{8,11},{9,8},{10,9... | collective-permute-start | bytes 884744 | tf_op jit(solution)/shard_map/ppermute | solution.py:541
  57.2 21.9 %copy-start = (bf16[192,768]{1,0:T(8,128)(2,1)}, bf16[192,768]{1,0:T(8,128)(2,1)S(1)}, u32[]{:S(2)}) copy-start(bf16[192,768]{1,0:T(8,128)(2,1)S(1)} %collective-permute-done.3.rest_1_) | copy-start | bytes 884740
  68.1 11.0 %copy-start.1 = (bf16[192,768]{1,0:T(8,128)(2,1)}, bf16[192,768]{1,0:T(8,128)(2,1)S(1)}, u32[]{:S(2)}) copy-start(bf16[192,768]{1,0:T(8,128)(2,1)S(1)} %collective-permute-done.4.rest_2_) | copy-start | bytes 884740
  68.1 11.0 %copy-start.3 = (bf16[192,768]{1,0:T(8,128)(2,1)}, bf16[192,768]{1,0:T(8,128)(2,1)S(1)}, u32[]{:S(2)}) copy-start(bf16[192,768]{1,0:T(8,128)(2,1)S(1)} %collective-permute-done.5.rest_3_) | copy-start | bytes 884740
  95.1 1.0 copy-start.11
  95.1 4.3 %copy-start.10 = (bf16[192,768]{1,0:T(8,128)(2,1)S(1)}, bf16[192,768]{1,0:T(8,128)(2,1)}, u32[]{:S(2)}) copy-start(bf16[192,768]{1,0:T(8,128)(2,1)} %get-tuple-element.33) | copy-start | bytes 884740
  95.1 4.3 %copy-start.9 = (bf16[192,768]{1,0:T(8,128)(2,1)S(1)}, bf16[192,768]{1,0:T(8,128)(2,1)}, u32[]{:S(2)}) copy-start(bf16[192,768]{1,0:T(8,128)(2,1)} %get-tuple-element.34) | copy-start | bytes 884740
  96.1 10.8 %collective-permute-start.6 = (bf16[192,768]{1,0:T(8,128)(2,1)S(1)}, bf16[192,768]{1,0:T(8,128)(2,1)S(1)}, u32[]{:S(2)}, u32[]{:S(2)}) collective-permute-start(bf16[192,768]{1,0:T(8,128)(2,1)S(1)} %copy-done.11), channel_id=1, source_target_pairs={{0,3},{1,0},{2,1},{3,2},{4,7},{5,4},{6,5},{7,6},{8,11},{9,8},{10,9... | collective-permute-start | bytes 884744 | tf_op jit(solution)/shard_map/ppermute | solution.py:541
  99.4 25.7 %collective-permute-start.7 = (bf16[192,768]{1,0:T(8,128)(2,1)S(1)}, bf16[192,768]{1,0:T(8,128)(2,1)S(1)}, u32[]{:S(2)}, u32[]{:S(2)}) collective-permute-start(bf16[192,768]{1,0:T(8,128)(2,1)S(1)} %copy-done.10), channel_id=1, source_target_pairs={{0,2},{1,3},{2,0},{3,1},{4,6},{5,7},{6,4},{7,5},{8,10},{9,11},{10,... | collective-permute-start | bytes 884744 | tf_op jit(solution)/shard_map/ppermute | solution.py:541
  99.4 25.7 %collective-permute-start.8 = (bf16[192,768]{1,0:T(8,128)(2,1)S(1)}, bf16[192,768]{1,0:T(8,128)(2,1)S(1)}, u32[]{:S(2)}, u32[]{:S(2)}) collective-permute-start(bf16[192,768]{1,0:T(8,128)(2,1)S(1)} %copy-done.9), channel_id=1, source_target_pairs={{0,1},{1,2},{2,3},{3,0},{4,5},{5,6},{6,7},{7,4},{8,9},{9,10},{10,1... | collective-permute-start | bytes 884744 | tf_op jit(solution)/shard_map/ppermute | solution.py:541
  106.8 18.3 %copy-start.2 = (bf16[192,768]{1,0:T(8,128)(2,1)}, bf16[192,768]{1,0:T(8,128)(2,1)S(1)}, u32[]{:S(2)}) copy-start(bf16[192,768]{1,0:T(8,128)(2,1)S(1)} %collective-permute-done.6.rest_1_) | copy-start | bytes 884740
  125.1 0.7 copy-start.4
  125.1 0.8 copy-start.5
  134.6 1.4 collective-permute-start.9
  137.0 8.1 %collective-permute-start.10 = (bf16[192,384]{1,0:T(8,128)(2,1)S(1)}, bf16[192,384]{1,0:T(8,128)(2,1)S(1)}, u32[]{:S(2)}, u32[]{:S(2)}) collective-permute-start(bf16[192,384]{1,0:T(8,128)(2,1)S(1)} %add_convert_fusion.1), channel_id=1, source_target_pairs={{0,8},{4,12},{8,0},{12,4},{16,24},{20,28},{24,16},{28,20},{1,9},{5... | collective-permute-start | bytes 442376 | tf_op jit(solution)/shard_map/ppermute | solution.py:550
  145.2 12.7 %collective-permute-start.11 = (bf16[192,384]{1,0:T(8,128)(2,1)S(1)}, bf16[192,384]{1,0:T(8,128)(2,1)S(1)}, u32[]{:S(2)}, u32[]{:S(2)}) collective-permute-start(bf16[192,384]{1,0:T(8,128)(2,1)S(1)} %add_convert_fusion), channel_id=1, source_target_pairs={{0,16},{4,20},{8,24},{12,28},{16,0},{20,4},{24,8},{28,12},{1,17},{... | collective-permute-start | bytes 442376 | tf_op jit(solution)/shard_map/ppermute | solution.py:550
  152.4 8.6 %collective-permute-start.14 = (bf16[4,48,384]{2,1,0:T(8,128)(2,1)S(1)}, bf16[4,48,384]{2,1,0:T(8,128)(2,1)S(1)}, u32[]{:S(2)}, u32[]{:S(2)}) collective-permute-start(bf16[4,48,384]{2,1,0:T(8,128)(2,1)S(1)} %get-tuple-element.39), channel_id=1, source_target_pairs={{0,1},{1,2},{2,3},{3,0},{4,5},{5,6},{6,7},{7,4},{8,9},{9,10},{10,1... | collective-permute-start | bytes 442376 | tf_op jit(solution)/shard_map/ppermute | solution.py:541
  155.1 11.3 %collective-permute-start.13 = (bf16[4,48,384]{2,1,0:T(8,128)(2,1)S(1)}, bf16[4,48,384]{2,1,0:T(8,128)(2,1)S(1)}, u32[]{:S(2)}, u32[]{:S(2)}) collective-permute-start(bf16[4,48,384]{2,1,0:T(8,128)(2,1)S(1)} %get-tuple-element.40), channel_id=1, source_target_pairs={{0,2},{1,3},{2,0},{3,1},{4,6},{5,7},{6,4},{7,5},{8,10},{9,11},{10,... | collective-permute-start | bytes 442376 | tf_op jit(solution)/shard_map/ppermute | solution.py:541
  156.1 10.3 %collective-permute-start.12 = (bf16[4,48,384]{2,1,0:T(8,128)(2,1)S(1)}, bf16[4,48,384]{2,1,0:T(8,128)(2,1)S(1)}, u32[]{:S(2)}, u32[]{:S(2)}) collective-permute-start(bf16[4,48,384]{2,1,0:T(8,128)(2,1)S(1)} %get-tuple-element.41), channel_id=1, source_target_pairs={{0,3},{1,0},{2,1},{3,2},{4,7},{5,4},{6,5},{7,6},{8,11},{9,8},{10,9... | collective-permute-start | bytes 442376 | tf_op jit(solution)/shard_map/ppermute | solution.py:541
  161.0 5.4 %copy-start.6 = (bf16[4,48,384]{2,1,0:T(8,128)(2,1)}, bf16[4,48,384]{2,1,0:T(8,128)(2,1)S(1)}, u32[]{:S(2)}) copy-start(bf16[4,48,384]{2,1,0:T(8,128)(2,1)S(1)} %collective-permute-done.14.rest_3_) | copy-start | bytes 442372
  166.4 0.7 copy-start.7
  166.4 0.7 copy-start.8
Sparse Core Ops, SparseCore 0:
  37.8 41.2 all-gather.2
  95.3 55.2 reduce-scatter.1

commit v3 on v2

--- a/solution.py
+++ b/solution.py
@@ -68,11 +68,12 @@
     w_out_ref,
     *rest,
     groups,
+    calls,
 ):
     send_refs = rest[:groups]
     gamma_ref, gate_ref, stage_ref = rest[groups:]
     width = stage_ref.shape[2]
-    part = width // 4
+    part = width // (4 * calls)
     group_own = group_ref[0]
     single_norm, _ = norm_rows(single_ref[...].astype(F32))
     single_b = single_norm.astype(BF16)
@@ -88,9 +89,10 @@
         rounded = values.astype(BF16)
         for group in range(groups):
             slot = lax.rem(group - group_own + groups, groups)
-            stage_ref[slot, :, kind * part : (kind + 1) * part] = rounded[
-                :, group * part : (group + 1) * part
-            ]
+            for call in range(calls):
+                feature = (group * calls + call) * part
+                lane = (call * 4 + kind) * part
+                stage_ref[slot, :, lane : lane + part] = rounded[:, feature : feature + part]
 
     put(0, mm(x_b, w_query_ref[...]))
     put(1, mm(x_b, w_key_ref[...]))
@@ -141,7 +143,7 @@
     group_own = group_ref[0]
     row_base = rows_ref[0] * 2 * half + pl.program_id(0) * step
     means = mean_matrix(channels)
-    weight = w_pair_ref[...].astype(F32).T.astype(BF16)
+    weight = w_pair_ref[...]
     left = jnp.concatenate(
         [
             jnp.concatenate([weight, jnp.zeros((heads, channels), BF16)], axis=1),
@@ -155,7 +157,10 @@
         ],
         axis=0,
     )
-    chain_cols = cols_ref[pl.ds(group_own, 1), :]
+    chain_cols = cols_ref[:, :cols]
+    for group in range(1, groups):
+        here = cols_ref[:, group * cols : (group + 1) * cols]
+        chain_cols = jnp.where(group_own == group, here, chain_cols)
     for head in range(heads):
         gains_ref[head : head + 1, :] = jnp.full((1, cols), gain_ref[head], F32)
 
@@ -217,8 +222,8 @@
             smem(),
             smem(),
             pl.BlockSpec((2, step, cols, channels), lambda t: (0, t, 0, 0)),
-            pl.BlockSpec((channels, heads), lambda t: (0, 0)),
-            pl.BlockSpec((groups, cols), lambda t: (0, 0)),
+            pl.BlockSpec((heads, channels), lambda t: (0, 0)),
+            pl.BlockSpec((1, groups * cols), lambda t: (0, 0)),
         ],
         out_specs=[
             pl.BlockSpec((per_group, step, 2 * cols), lambda t: (0, t, 0)) for _ in range(groups)
@@ -240,21 +245,23 @@
         chains,
         chain_gain,
         pair.reshape(2, half, cols, channels),
-        w_pair,
-        chains.reshape(groups, cols),
+        w_pair.T,
+        chains.reshape(1, groups * cols),
     )
     return sends, stats
 
 
-def pair_back_kernel(group_ref, pair_ref, stats_ref, w_pair_ref, *rest, groups, factor, batch):
-    grad_refs = rest[:groups]
-    out_ref, flat_ref = rest[groups:]
+def pair_back_kernel(
+    group_ref, pair_ref, stats_ref, w_pair_ref, *rest, groups, calls, factor, batch
+):
+    grad_refs = rest[: groups * calls]
+    out_ref, flat_ref = rest[groups * calls :]
     _, step, cols, channels = pair_ref.shape
-    per_group = grad_refs[0].shape[0]
-    heads = groups * per_group
+    per_call = grad_refs[0].shape[0]
+    heads = groups * calls * per_call
     group_own = group_ref[0]
     means = mean_matrix(channels)
-    weight = w_pair_ref[...].astype(F32).T
+    weight = w_pair_ref[...].astype(F32)
     weight = weight - jnp.mean(weight, axis=-1, keepdims=True)
     high = weight.astype(BF16)
     low = (weight - high.astype(F32)).astype(BF16)
@@ -263,11 +270,12 @@
     spread = ((spread >= 2 * heads) & (spread < 2 * heads + 2)).astype(F32).astype(BF16)
     weights = jnp.concatenate([weights, spread], axis=1)
     blank = jnp.zeros((14, cols), F32)
-    for slot in range(groups):
-        source = lax.rem(group_own + slot, groups)
-        for head in range(per_group):
-            values = grad_refs[slot][head].astype(F32)
-            top = pl.multiple_of((source * per_group + head) * step, step)
+    for number in range(groups * calls):
+        call, slot = divmod(number, groups)
+        source = lax.rem(group_own + slot, groups) * calls + call
+        for head in range(per_call):
+            values = grad_refs[number][head].astype(F32)
+            top = pl.multiple_of((source * per_call + head) * step, step)
             for side in range(2):
                 for tile, start, end in lane_tiles(cols):
                     flat_ref[side, tile, pl.ds(top, step), : end - start] = values[
@@ -312,37 +320,41 @@
     lax.fori_loop(0, step // batch, some_rows, 0)
 
 
-def pair_back(pair, stats, grads, w_pair, group_index, factor):
+def pair_back(pair, stats, grads, w_pair, group_index, groups, factor):
     rows, cols, channels = pair.shape
-    groups = len(grads)
-    per_group = grads[0].shape[0]
-    heads = groups * per_group
+    per_call = grads[0].shape[0]
+    heads = len(grads) * per_call
     half = rows // 2
     step = 16
     tiles = -(-cols // 128)
     out = pl.pallas_call(
-        functools.partial(pair_back_kernel, groups=groups, factor=factor, batch=4),
+        functools.partial(
+            pair_back_kernel, groups=groups, calls=len(grads) // groups, factor=factor, batch=4
+        ),
         grid=(half // step,),
         in_specs=[
             smem(),
             pl.BlockSpec((2, step, cols, channels), lambda t: (0, t, 0, 0)),
             pl.BlockSpec((2, step, heads + 8, cols), lambda t: (0, t, 0, 0)),
-            pl.BlockSpec((channels, heads), lambda t: (0, 0)),
+            pl.BlockSpec((heads, channels), lambda t: (0, 0)),
         ]
-        + [pl.BlockSpec((per_group, step, 2 * cols), lambda t: (0, t, 0)) for _ in range(groups)],
+        + [pl.BlockSpec((per_call, step, 2 * cols), lambda t: (0, t, 0)) for _ in grads],
         out_specs=pl.BlockSpec((2, step, cols, channels), lambda t: (0, t, 0, 0)),
         out_shape=jax.ShapeDtypeStruct((2, half, cols, channels), BF16),
         scratch_shapes=[pltpu.VMEM((2, tiles, heads * step, 128), F32)],
         compiler_params=params(),
-    )(group_index, pair.reshape(2, half, cols, channels), stats, w_pair, *grads)
+    )(group_index, pair.reshape(2, half, cols, channels), stats, w_pair.T, *grads)
     return out.reshape(rows, cols, channels)
 
 
-def attention_kernel(group_ref, bias_ref, *rest, groups, head_size, row_block):
-    acts_refs = rest[:groups]
-    out_refs = rest[groups : 2 * groups]
+def attention_kernel(group_ref, row_ref, *rest, groups, row_parts, head_size, row_block):
+    bias_refs = rest[:row_parts]
+    acts_refs = rest[row_parts : row_parts + groups]
+    rest = rest[row_parts + groups :]
+    out_refs = rest[:groups]
     (
-        dbias_ref,
+        keep_ref,
+        give_ref,
         query_ref,
         keys_ref,
         values_ref,
@@ -357,15 +369,14 @@
         gq_sum,
         gk_sum,
         gv_sum,
-    ) = rest[2 * groups :]
+    ) = rest[groups:]
     head = pl.program_id(0)
     heads = pl.num_programs(0)
     group_own = group_ref[0]
     cols, width = acts_refs[0].shape
     tokens = groups * cols
     part = width // 4
-    row_parts = bias_ref.shape[0]
-    half = bias_ref.shape[3]
+    half = bias_refs[0].shape[2]
     scale = 1.0 / math.sqrt(head_size)
     extra = att_sum.shape[1] - part
     plain = (query_ref, keys_ref, values_ref, grads_ref)
@@ -383,17 +394,18 @@
         gq_sum[...] = jnp.zeros_like(gq_sum)
 
     def places():
-        for row_part in range(row_parts):
-            owner, inside = divmod(row_part * 2 * half, cols)
-            slot = lax.rem(group_own - owner + groups, groups)
+        for other in range(row_parts):
+            first = (row_ref[0] ^ other) * (2 * half)
+            slot = lax.rem(group_own - first // cols + groups, groups)
             for side in range(2):
-                top = pl.multiple_of(slot * cols + inside + side * half, 16)
+                top = slot * cols + lax.rem(first, cols) + side * half
+                top = pl.multiple_of(top, 16)
                 for column in range(groups):
-                    yield row_part, column, side, pl.ds(top, half)
-
-    for row_part, column, side, rows in places():
-        bias_full[rows, column * cols : (column + 1) * cols] = bias_ref[
-            row_part, column, 0, :, side * cols : (side + 1) * cols
+                    yield other, column, side, pl.ds(top, half)
+
+    for other, column, side, rows in places():
+        bias_full[rows, column * cols : (column + 1) * cols] = bias_refs[other][
+            column, 0, :, side * cols : (side + 1) * cols
         ]
 
     lane = lax.broadcasted_iota(jnp.int32, (1, part), 1)
@@ -429,8 +441,9 @@
     gk_sum[pl.ds(feature, head_size), :] = gk_t
     gv_sum[pl.ds(feature, head_size), :] = gv_t
 
-    for row_part, column, side, rows in places():
-        dbias_ref[row_part, column, 0, :, side * cols : (side + 1) * cols] = score_full[
+    for other, column, side, rows in places():
+        dbias_ref = give_ref if other % 2 else keep_ref
+        dbias_ref[other // 2, column, 0, :, side * cols : (side + 1) * cols] = score_full[
             rows, column * cols : (column + 1) * cols
         ]
 
@@ -450,25 +463,38 @@
                 ]
 
 
-def attention(group_index, acts, bias, head_size):
+def attention(group_index, row_index, acts, bias, head_size, call, calls):
     groups = len(acts)
+    row_parts = len(bias)
     cols, width = acts[0].shape
+    width = width // calls
     tokens = groups * cols
     part = width // 4
-    row_parts, _, heads, half, lanes = bias.shape
+    _, heads, half, lanes = bias[0].shape
+    heads = heads // calls
     row_block = 256 if tokens % 256 == 0 else cols
-    spread = (row_parts, groups, 1, half, lanes)
     padded = (part // 128 + 1) * 128
-    slots = [pl.BlockSpec((cols, width), lambda h: (0, 0)) for _ in range(groups)]
-    *grads, dbias = pl.pallas_call(
+    halves = (row_parts // 2, groups, heads, half, lanes)
+    *grads, keep, give = pl.pallas_call(
         functools.partial(
-            attention_kernel, groups=groups, head_size=head_size, row_block=row_block
+            attention_kernel,
+            groups=groups,
+            row_parts=row_parts,
+            head_size=head_size,
+            row_block=row_block,
         ),
         grid=(heads,),
-        in_specs=[smem(), pl.BlockSpec(spread, lambda h: (0, 0, h, 0, 0))] + slots,
-        out_specs=slots + [pl.BlockSpec(spread, lambda h: (0, 0, h, 0, 0))],
-        out_shape=[jax.ShapeDtypeStruct((cols, width), BF16) for _ in range(groups)]
-        + [jax.ShapeDtypeStruct(bias.shape, BF16)],
+        in_specs=[smem(), smem()]
+        + [pl.BlockSpec((groups, 1, half, lanes), lambda h: (0, call * heads + h, 0, 0))]
+        * row_parts
+        + [pl.BlockSpec((cols, width), lambda h: (0, call))] * groups,
+        out_specs=[pl.BlockSpec((cols, width), lambda h: (0, 0))] * groups
+        + [
+            pl.BlockSpec((row_parts // 2, groups, 1, half, lanes), lambda h: (0, 0, h, 0, 0))
+        ]
+        * 2,
+        out_shape=[jax.ShapeDtypeStruct((cols, width), BF16)] * groups
+        + [jax.ShapeDtypeStruct(halves, BF16)] * 2,
         scratch_shapes=[pltpu.VMEM((tokens, part), BF16) for _ in range(4)]
         + [pltpu.VMEM((part, tokens), BF16) for _ in range(4)]
         + [
@@ -480,8 +506,8 @@
             pltpu.VMEM((part, tokens), F32),
         ],
         compiler_params=params(),
-    )(group_index, bias, *acts)
-    return grads, dbias
+    )(group_index, row_index, *bias, *acts)
+    return grads, keep, give
 
 
 def finish_kernel(
@@ -500,17 +526,25 @@
     w_out_ref,
     *rest,
     groups,
+    calls,
 ):
-    got_refs = rest[:groups]
-    updated_ref, d_single_ref, stage_ref = rest[groups:]
-    width = stage_ref.shape[2]
+    got_refs = rest[: groups * calls]
+    updated_ref, d_single_ref, stage_ref = rest[groups * calls :]
+    width = stage_ref.shape[3]
     part = width // 4
     for slot in range(groups):
-        stage_ref[lax.rem(group_ref[0] + slot, groups)] = got_refs[slot][...]
+        for call in range(calls):
+            stage_ref[lax.rem(group_ref[0] + slot, groups), call] = got_refs[
+                call * groups + slot
+            ][...]
 
     def take(kind):
         return jnp.concatenate(
-            [stage_ref[group, :, kind * part : (kind + 1) * part] for group in range(groups)],
+            [
+                stage_ref[group, call, :, kind * part : (kind + 1) * part]
+                for group in range(groups)
+                for call in range(calls)
+            ],
             axis=1,
         )
 
@@ -542,12 +576,32 @@
     return got
 
 
+def flip_rows(values, bits, row_total):
+    return lax.ppermute(values, "rows", [(index, index ^ bits) for index in range(row_total)])
+
+
+def gather_rows(own, row_total):
+    blocks = [None] * row_total
+    for bits in range(0, row_total, 2):
+        blocks[bits] = flip_rows(own, bits, row_total) if bits else own
+    for bits in range(0, row_total, 2):
+        blocks[bits + 1] = flip_rows(blocks[bits], 1, row_total)
+    return blocks
+
+
+def scatter_rows(keep, give, row_total):
+    both = keep.astype(F32) + flip_rows(give, 1, row_total).astype(F32)
+    total = both[0]
+    for bits in range(2, row_total, 2):
+        total += flip_rows(both[bits // 2].astype(BF16), bits, row_total).astype(F32)
+    return total.astype(BF16)
+
+
 def sum_rows(values, row_total):
     bit = 1
     while bit < row_total:
-        perm = [(index, index ^ bit) for index in range(row_total)]
         mine = values.astype(BF16)
-        values = mine.astype(F32) + lax.ppermute(mine, "rows", perm).astype(F32)
+        values = mine.astype(F32) + flip_rows(mine, bit, row_total).astype(F32)
         bit *= 2
     return values
 
@@ -575,17 +629,17 @@
     tokens = chains.shape[0]
     width = noised.shape[2]
     head_size = width // w_pair.shape[1]
+    calls = 2
     row_index = lax.axis_index("rows").reshape(1)
     group_index = lax.axis_index("grp").reshape(1)
     bias_send, stats = pair_bias(
         pair, w_pair, chain_gain, chains, group_index, row_index, groups
     )
-    bias_own = jnp.stack(swap_groups(bias_send, 1))
-    bias_all = lax.all_gather(bias_own, "rows", axis=0)
+    bias_got = swap_groups(bias_send, 1)
     noised = noised[0]
     cotangent = cotangent[0]
     *acts_send, cond_gamma, out_gate = pl.pallas_call(
-        functools.partial(project_kernel, groups=groups),
+        functools.partial(project_kernel, groups=groups, calls=calls),
         in_specs=[smem()] + [vmem()] * 10,
         out_shape=[
             jax.ShapeDtypeStruct((cols, 4 * width // groups), BF16) for _ in range(groups)
@@ -609,19 +663,26 @@
         w_value,
         w_out,
     )
+    bias_got, acts_send = lax.optimization_barrier((bias_got, acts_send))
     acts = swap_groups(acts_send, 1)
-    grads_send, dbias = attention(group_index, acts, bias_all, head_size)
-    grads = swap_groups(grads_send, -1)
-    dbias_own = lax.psum_scatter(dbias, "rows", scatter_dimension=0, tiled=False)
-    dbias_back = swap_groups([dbias_own[slot] for slot in range(groups)], -1)
+    bias_all = gather_rows(jnp.stack(bias_got), row_total)
+    grads = []
+    dbias_back = []
+    for call in range(calls):
+        grads_send, keep, give = attention(
+            group_index, row_index, acts, bias_all, head_size, call, calls
+        )
+        dbias_own = scatter_rows(keep, give, row_total)
+        grads.append(swap_groups(grads_send, -1))
+        dbias_back += swap_groups([dbias_own[slot] for slot in range(groups)], -1)
     updated, d_part = pl.pallas_call(
-        functools.partial(finish_kernel, groups=groups),
-        in_specs=[smem()] + [vmem()] * (12 + groups),
+        functools.partial(finish_kernel, groups=groups, calls=calls),
+        in_specs=[smem()] + [vmem()] * (12 + groups * calls),
         out_shape=[
             jax.ShapeDtypeStruct((cols, width), BF16),
             jax.ShapeDtypeStruct(single.shape, F32),
         ],
-        scratch_shapes=[pltpu.VMEM((groups, cols, 4 * width // groups), BF16)],
+        scratch_shapes=[pltpu.VMEM((groups, calls, cols, 4 * width // (groups * calls)), BF16)],
         compiler_params=params(),
     )(
         group_index,
@@ -637,10 +698,11 @@
         w_key,
         w_value,
         w_out,
-        *grads,
+        *grads[0],
+        *grads[1],
     )
     d_single = sum_rows(d_part, row_total)
-    d_pair = pair_back(pair, stats, dbias_back, w_pair, group_index, float(tokens))
+    d_pair = pair_back(pair, stats, dbias_back, w_pair, group_index, groups, float(tokens))
     return (updated[None], d_single, d_pair)
 
 
@@ -806,7 +868,7 @@
             and row_total == 8
             and noised.shape[0] == 1
             and noised.shape[1] % 64 == 0
-            and w_pair.shape[1] % groups == 0
+            and w_pair.shape[1] % (2 * groups) == 0
         )
         if fits:
             return split_heads(*args, groups=groups, row_total=row_total)

time: 185 us -> 180 us (0.973)
  starting transfers between devices: 25.8 us -> 45.7 us
  waiting for transfers between devices: 81.9 us -> 68.2 us
  between operations: 14.1 us -> 0.97 us
  Pallas kernels: 50.1 us -> 54.2 us
    ppermute x3 -> x18, waiting for transfers between devices: 7.96 us -> 36.5 us  [flip_rows(): lax.ppermute(values, 'rows', [(index, index ^ bits) for index in range(ro...]
    ppermute x12 -> x18, waiting for transfers between devices: 58.7 us -> 31.7 us  [swap_groups(): got.append(lax.ppermute(sends[shift], 'grp', perm))]
    ppermute x3 -> x18, starting transfers between devices: 2.72 us -> 15.1 us  [flip_rows(): lax.ppermute(values, 'rows', [(index, index ^ bits) for index in range(ro...]
    all_gather x1 -> x0, waiting for transfers between devices: 11 us -> none  [split_heads(): bias_all = lax.all_gather(bias_own, 'rows', axis=0)]
    ppermute x12 -> x18, starting transfers between devices: 23 us -> 30.6 us  [swap_groups(): got.append(lax.ppermute(sends[shift], 'grp', perm))]
    reduce_scatter x1 -> x0, waiting for transfers between devices: 4.19 us -> none  [split_heads(): lax.psum_scatter(dbias, 'rows', scatter_dimension=0, tiled=False)]
    pallas_call x4 -> x5, Pallas kernels: 39.8 us -> 43.4 us  [the longest x2 19.6 us: attention(): pl.pallas_call(functools.partial(attention_kernel, groups=groups, row_par...]
    unnamed x25 -> x60, local copies, waits for them, and re-layouts: 3.88 us -> 3.43 us
  transfers between devices with their start and end apart: 17 -> 36, of which waited for: 12 -> 17; matrix products, arithmetic and copies ran while one was open for 3% -> 3% of each run, Pallas kernels for 8% -> 13%
where the time goes in v3:
time: 180 us; the launch traced here: 179 us
  waiting for transfers between devices  68.2 us (38%)
  Pallas kernels  54.2 us (30%)
  starting transfers between devices  45.7 us (25%)
  local copies, waits for them, and re-layouts  6.19 us (3%)
  other arithmetic  3.98 us (2%)
    ppermute x18, waiting for transfers between devices, flip_rows(): lax.ppermute(values, 'rows', [(index, index ^ bits) for index in range(ro...  36.5 us
    ppermute x18, waiting for transfers between devices, swap_groups(): got.append(lax.ppermute(sends[shift], 'grp', perm))  31.7 us
    ppermute x18, starting transfers between devices, swap_groups(): got.append(lax.ppermute(sends[shift], 'grp', perm))  30.6 us
    pallas_call x2, Pallas kernels, attention(): pl.pallas_call(functools.partial(attention_kernel, groups=groups, row_par...  19.6 us
    ppermute x18, starting transfers between devices, flip_rows(): lax.ppermute(values, 'rows', [(index, index ^ bits) for index in range(ro...  15.1 us
    pallas_call x1, Pallas kernels, pair_bias(): pl.pallas_call(functools.partial(bias_kernel, groups=groups, batch=4), gr...  10.8 us
    pallas_call x1, Pallas kernels, pair_back(): pl.pallas_call(functools.partial(pair_back_kernel, groups=groups, calls=l...  9.66 us
    pallas_call x1, Pallas kernels, split_heads(): pl.pallas_call(functools.partial(finish_kernel, groups=groups, calls=call...  7.65 us
  transfers between devices with their start and end apart: 36, of which 17 were waited for; matrix products, arithmetic and copies ran while one was open for 3% of the time, Pallas kernels for 13%

profile of v3, /device:TPU:0, one launch (start us, length us, event | category | flops | bytes accessed | tf_op | source)
XLA Modules:
  0.0 179.3 jit_solution(10766148525018644908)
XLA Ops:
  0.6 1.3 reshape.31.cols_ref
  1.9 10.8 %shard_map.158 = (bf16[4,48,384]{2,1,0:T(8,128)(2,1)}, bf16[4,48,384]{2,1,0:T(8,128)(2,1)}, bf16[4,48,384]{2,1,0:T(8,128)(2,1)}, bf16[4,48,384]{2,1,0:T(8,128)(2,1)}, f32[2,48,24,192]{3,2,1,0:T(8,128)}) custom-call(s32[1]{0:T(128)} %bitcast.group_ref, s32[1]{0:T(128)} %bitcast.3.rows_ref.row_ref, s32[768]{0:T(1024)} %chains_ref.1, f32[16]{0:T(128)} %gain_ref.1, ...), custom_call_target="tpu_custom_call" | custom-call | tf_op jit(solution)/shard_map/pallas_call | solution.py:216
  12.7 3.0 %collective-permute-start = (bf16[4,48,384]{2,1,0:T(8,128)(2,1)}, bf16[4,48,384]{2,1,0:T(8,128)(2,1)S(1)}, u32[]{:S(2)}, u32[]{:S(2)}) collective-permute-start(bf16[4,48,384]{2,1,0:T(8,128)(2,1)} %get-tuple-element.39), channel_id=1, source_target_pairs={{0,1},{1,2},{2,3},{3,0},{4,5},{5,6},{6,7},{7,4},{8,9},{9,10},{10,1... | collective-permute-start | bytes 442376 | tf_op jit(solution)/shard_map/ppermute | solution.py:575
  15.7 2.6 %collective-permute-start.1 = (bf16[4,48,384]{2,1,0:T(8,128)(2,1)}, bf16[4,48,384]{2,1,0:T(8,128)(2,1)S(1)}, u32[]{:S(2)}, u32[]{:S(2)}) collective-permute-start(bf16[4,48,384]{2,1,0:T(8,128)(2,1)} %get-tuple-element.40), channel_id=1, source_target_pairs={{0,2},{1,3},{2,0},{3,1},{4,6},{5,7},{6,4},{7,5},{8,10},{9,11},{10,... | collective-permute-start | bytes 442376 | tf_op jit(solution)/shard_map/ppermute | solution.py:575
  18.3 1.3 collective-permute-start.2
  19.7 6.5 %shard_map.157 = (bf16[192,768]{1,0:T(8,128)(2,1)}, bf16[192,768]{1,0:T(8,128)(2,1)}, bf16[192,768]{1,0:T(8,128)(2,1)}, bf16[192,768]{1,0:T(8,128)(2,1)}, f32[192,768]{1,0:T(8,128)}, /*index=5*/f32[192,768]{1,0:T(8,128)}) custom-call(s32[1]{0:T(128)} %bitcast.group_ref, bf16[192,384]{1,0:T(8,128)(2,1)} %single_ref.3, bf16[192,768]{1,0:T(8,128)(2,1)} %bitcast.63, ...), custom_call_target="tpu_custom_call" | custom-call | tf_op jit(solution)/shard_map/pallas_call | solution.py:641
  26.2 2.0 %collective-permute-done.1 = bf16[4,48,384]{2,1,0:T(8,128)(2,1)S(1)} collective-permute-done((bf16[4,48,384]{2,1,0:T(8,128)(2,1)}, bf16[4,48,384]{2,1,0:T(8,128)(2,1)S(1)}, u32[]{:S(2)}, u32[]{:S(2)}) %collective-permute-start.1) | collective-permute-done | bytes 147488 | tf_op jit(solution)/shard_map/ppermute | solution.py:575
  28.3 2.5 %collective-permute-start.8 = (bf16[4,4,48,384]{3,2,1,0:T(8,128)(2,1)S(1)}, bf16[4,4,48,384]{3,2,1,0:T(8,128)(2,1)S(1)}, u32[]{:S(2)}, u32[]{:S(2)}) collective-permute-start(bf16[4,4,48,384]{3,2,1,0:T(8,128)(2,1)S(1)} %pad_maximum_fusion.rest_0_), channel_id=1, source_target_pairs={{0,24},{4,28},{8,16},{12,20},{16,8},{20,12},{24,0},{28,4},{1,25},{... | collective-permute-start | bytes 1769480 | tf_op jit(solution)/shard_map/ppermute | solution.py:580
  30.8 0.5 collective-permute-start.6
  31.3 0.5 collective-permute-start.4
  31.9 3.6 %collective-permute-start.10 = (bf16[192,768]{1,0:T(8,128)(2,1)S(1)}, bf16[192,768]{1,0:T(8,128)(2,1)S(1)}, u32[]{:S(2)}, u32[]{:S(2)}) collective-permute-start(bf16[192,768]{1,0:T(8,128)(2,1)S(1)} %copy-done.29), channel_id=1, source_target_pairs={{0,1},{1,2},{2,3},{3,0},{4,5},{5,6},{6,7},{7,4},{8,9},{9,10},{10,1... | collective-permute-start | bytes 884744 | tf_op jit(solution)/shard_map/ppermute | solution.py:575
  35.5 1.6 collective-permute-start.11
  37.1 7.5 %collective-permute-done.10.rest_9_ = bf16[192,768]{1,0:T(8,128)(2,1)S(1)} collective-permute-done((bf16[192,768]{1,0:T(8,128)(2,1)S(1)}, bf16[192,768]{1,0:T(8,128)(2,1)S(1)}, u32[]{:S(2)}, u32[]{:S(2)}) %collective-permute-start.10) | collective-permute-done | bytes 294944 | tf_op jit(solution)/shard_map/ppermute | solution.py:575
  44.6 0.9 collective-permute-done.8.rest_6_
  45.5 11.5 %collective-permute-done.6.rest_4_ = bf16[4,4,48,384]{3,2,1,0:T(8,128)(2,1)S(1)} collective-permute-done((bf16[4,4,48,384]{3,2,1,0:T(8,128)(2,1)S(1)}, bf16[4,4,48,384]{3,2,1,0:T(8,128)(2,1)S(1)}, u32[]{:S(2)}, u32[]{:S(2)}) %collective-permute-start.6) | collective-permute-done | bytes 589856 | tf_op jit(solution)/shard_map/ppermute | solution.py:580
  57.2 0.4 collective-permute-start.5
  57.6 3.8 %collective-permute-start.12 = (bf16[192,768]{1,0:T(8,128)(2,1)S(1)}, bf16[192,768]{1,0:T(8,128)(2,1)S(1)}, u32[]{:S(2)}, u32[]{:S(2)}) collective-permute-start(bf16[192,768]{1,0:T(8,128)(2,1)S(1)} %copy-done.27), channel_id=1, source_target_pairs={{0,3},{1,0},{2,1},{3,2},{4,7},{5,4},{6,5},{7,6},{8,11},{9,8},{10,9... | collective-permute-start | bytes 884744 | tf_op jit(solution)/shard_map/ppermute | solution.py:575
  61.4 7.3 %collective-permute-done.12.rest_11_ = bf16[192,768]{1,0:T(8,128)(2,1)S(1)} collective-permute-done((bf16[192,768]{1,0:T(8,128)(2,1)S(1)}, bf16[192,768]{1,0:T(8,128)(2,1)S(1)}, u32[]{:S(2)}, u32[]{:S(2)}) %collective-permute-start.12) | collective-permute-done | bytes 294944 | tf_op jit(solution)/shard_map/ppermute | solution.py:575
  68.8 0.6 copy-done.10
  69.4 0.2 copy-done.4
  69.6 0.2 copy-done.5
  69.8 0.2 copy-done.6
  70.0 0.8 copy-done.7
  70.8 9.8 %shard_map.160 = (bf16[192,384]{1,0:T(8,128)(2,1)}, bf16[192,384]{1,0:T(8,128)(2,1)}, bf16[192,384]{1,0:T(8,128)(2,1)}, bf16[192,384]{1,0:T(8,128)(2,1)}, bf16[4...) custom-call(s32[1]{0:T(128)} %bitcast.group_ref, s32[1]{0:T(128)} %bitcast.3.rows_ref.row_ref, ...), custom_call_target="tpu_custom_call" | custom-call | tf_op jit(solution)/shard_map/pallas_call | solution.py:478
  80.7 3.6 %collective-permute-start.16 = (bf16[192,384]{1,0:T(8,128)(2,1)}, bf16[192,384]{1,0:T(8,128)(2,1)S(1)}, u32[]{:S(2)}, u32[]{:S(2)}) collective-permute-start(bf16[192,384]{1,0:T(8,128)(2,1)} %get-tuple-element.59), channel_id=1, source_target_pairs={{0,3},{1,0},{2,1},{3,2},{4,7},{5,4},{6,5},{7,6},{8,11},{9,8},{10,9... | collective-permute-start | bytes 442376 | tf_op jit(solution)/shard_map/ppermute | solution.py:575
  84.3 0.7 collective-permute-start.18
  85.0 9.8 %shard_map.159 = (bf16[192,384]{1,0:T(8,128)(2,1)}, bf16[192,384]{1,0:T(8,128)(2,1)}, bf16[192,384]{1,0:T(8,128)(2,1)}, bf16[192,384]{1,0:T(8,128)(2,1)}, bf16[4...) custom-call(s32[1]{0:T(128)} %bitcast.group_ref, s32[1]{0:T(128)} %bitcast.3.rows_ref.row_ref, ...), custom_call_target="tpu_custom_call" | custom-call | tf_op jit(solution)/shard_map/pallas_call | solution.py:478
  94.7 3.4 %collective-permute-start.13 = (bf16[192,384]{1,0:T(8,128)(2,1)}, bf16[192,384]{1,0:T(8,128)(2,1)S(1)}, u32[]{:S(2)}, u32[]{:S(2)}) collective-permute-start(bf16[192,384]{1,0:T(8,128)(2,1)} %get-tuple-element.55), channel_id=1, source_target_pairs={{0,3},{1,0},{2,1},{3,2},{4,7},{5,4},{6,5},{7,6},{8,11},{9,8},{10,9... | collective-permute-start | bytes 442376 | tf_op jit(solution)/shard_map/ppermute | solution.py:575
  98.1 1.1 collective-permute-start.14
  99.3 3.5 %collective-permute-done.13.rest_1_ = bf16[192,384]{1,0:T(8,128)(2,1)S(1)} collective-permute-done((bf16[192,384]{1,0:T(8,128)(2,1)}, bf16[192,384]{1,0:T(8,128)(2,1)S(1)}, u32[]{:S(2)}, u32[]{:S(2)}) %collective-permute-start.13) | collective-permute-done | bytes 147488 | tf_op jit(solution)/shard_map/ppermute | solution.py:575
  102.7 9.5 %collective-permute-done.14.rest_2_ = bf16[192,384]{1,0:T(8,128)(2,1)S(1)} collective-permute-done((bf16[192,384]{1,0:T(8,128)(2,1)}, bf16[192,384]{1,0:T(8,128)(2,1)S(1)}, u32[]{:S(2)}, u32[]{:S(2)}) %collective-permute-start.14) | collective-permute-done | bytes 147488 | tf_op jit(solution)/shard_map/ppermute | solution.py:575
  112.3 0.6 copy-done.18
  113.0 7.7 %shard_map.161 = (bf16[192,768]{1,0:T(8,128)(2,1)}, f32[192,384]{1,0:T(8,128)}) custom-call(s32[1]{0:T(128)} %bitcast.group_ref, bf16[192,384]{1,0:T(8,128)(2,1)} %single_ref.3, bf16[192,768]{1,0:T(8,128)(2,1)} %bitcast.64, bf16[192,768]{1,0:T(8,128)(2,1)} %bitcast.66, f32[192,768]{1,0:T(8,128)} %get-tuple-element.36.gamma_ref, ...), custom_call_target="tpu_custom_call" | custom-call | tf_op jit(solution)/shard_map/pallas_call | solution.py:678
  120.7 1.1 convert_element_type.87
  121.8 0.5 collective-permute-start.22
  122.3 0.9 collective-permute-done.19
  123.2 1.0 add_convert_fusion.1
  124.2 1.6 collective-permute-start.20
  125.7 4.4 %collective-permute-done.20 = bf16[192,384]{1,0:T(8,128)(2,1)S(1)} collective-permute-done((bf16[192,384]{1,0:T(8,128)(2,1)S(1)}, bf16[192,384]{1,0:T(8,128)(2,1)S(1)}, u32[]{:S(2)}, u32[]{:S(2)}) %collective-permute-start.20) | collective-permute-done | bytes 147488 | tf_op jit(solution)/shard_map/ppermute | solution.py:580
  130.2 1.6 collective-permute-start.21
  131.8 0.4 fusion.9
  132.3 0.8 collective-permute-start.30
  133.1 1.2 collective-permute-start.32
  134.3 1.5 collective-permute-start.31
  135.8 0.4 fusion.8
  136.3 0.8 collective-permute-start.23
  137.2 5.1 %collective-permute-done.30 = bf16[4,2,48,384]{3,2,1,0:T(8,128)(2,1)S(1)} collective-permute-done((bf16[4,2,48,384]{3,2,1,0:T(8,128)(2,1)S(1)}, bf16[4,2,48,384]{3,2,1,0:T(8,128)(2,1)S(1)}, u32[]{:S(2)}, u32[]{:S(2)}) %collective-permute-start.30) | collective-permute-done | bytes 294944 | tf_op jit(solution)/shard_map/ppermute | solution.py:580
  142.3 1.4 collective-permute-start.25
  143.7 4.9 %collective-permute-done.32 = bf16[4,2,48,384]{3,2,1,0:T(8,128)(2,1)S(1)} collective-permute-done((bf16[4,2,48,384]{3,2,1,0:T(8,128)(2,1)S(1)}, bf16[4,2,48,384]{3,2,1,0:T(8,128)(2,1)S(1)}, u32[]{:S(2)}, u32[]{:S(2)}) %collective-permute-start.32) | collective-permute-done | bytes 294944 | tf_op jit(solution)/shard_map/ppermute | solution.py:580
  148.6 1.5 collective-permute-start.24
  150.2 0.6 slice_bitcast_fusion.8
  150.9 4.1 %collective-permute-done.23 = bf16[4,2,48,384]{3,2,1,0:T(8,128)(2,1)S(1)} collective-permute-done((bf16[4,2,48,384]{3,2,1,0:T(8,128)(2,1)S(1)}, bf16[4,2,48,384]{3,2,1,0:T(8,128)(2,1)S(1)}, u32[]{:S(2)}, u32[]{:S(2)}) %collective-permute-start.23) | collective-permute-done | bytes 294944 | tf_op jit(solution)/shard_map/ppermute | solution.py:580
  155.0 1.4 collective-permute-start.34
  156.4 2.9 %collective-permute-done.25 = bf16[4,2,48,384]{3,2,1,0:T(8,128)(2,1)S(1)} collective-permute-done((bf16[4,2,48,384]{3,2,1,0:T(8,128)(2,1)S(1)}, bf16[4,2,48,384]{3,2,1,0:T(8,128)(2,1)S(1)}, u32[]{:S(2)}, u32[]{:S(2)}) %collective-permute-start.25) | collective-permute-done | bytes 294944 | tf_op jit(solution)/shard_map/ppermute | solution.py:580
  159.4 1.7 collective-permute-done.24
  161.2 0.6 slice_bitcast_fusion.12
  161.8 0.4 collective-permute-start.28
  162.2 1.5 collective-permute-start.27
  163.6 2.6 %collective-permute-start.26 = (bf16[2,48,384]{2,1,0:T(8,128)(2,1)S(1)}, bf16[2,48,384]{2,1,0:T(8,128)(2,1)S(1)}, u32[]{:S(2)}, u32[]{:S(2)}) collective-permute-start(bf16[2,48,384]{2,1,0:T(8,128)(2,1)S(1)} %get-tuple-element.85), channel_id=1, source_target_pairs={{0,3},{1,0},{2,1},{3,2},{4,7},{5,4},{6,5},{7,6},{8,11},{9,8},{10,9... | collective-permute-start | bytes 221192 | tf_op jit(solution)/shard_map/ppermute | solution.py:575
  166.2 0.7 convert_add_fusion.2
  167.0 1.1 collective-permute-done.28.rest_3_
  168.1 0.9 collective-permute-done.27.rest_2_
  169.0 0.6 copy-done.24
  169.7 9.7 %shard_map.162 = bf16[2,48,192,128]{3,2,1,0:T(8,128)(2,1)} custom-call(s32[1]{0:T(128)} %bitcast.group_ref, bf16[2,48,192,128]{3,2,1,0:T(8,128)(2,1)} %bitcast.61, f32[2,48,24,192]{3,2,1,0:T(8,128)} %get-tuple-element.64.stats_ref, bf16[16,128]{1,0:T(8,128)(2,1)} %bitcast.72, bf16[2,48,384]{2,1,0:T(8,128)(2,1)} %get-tuple-element.86.rest_0_, ...), custom_call_target="tpu_custom_call" | custom-call | tf_op jit(solution)/shard_map/pallas_call | solution.py:330
  (88 shorter events, 1.1 us)
Async XLA Ops:
  12.7 13.5 %collective-permute-start = (bf16[4,48,384]{2,1,0:T(8,128)(2,1)}, bf16[4,48,384]{2,1,0:T(8,128)(2,1)S(1)}, u32[]{:S(2)}, u32[]{:S(2)}) collective-permute-start(bf16[4,48,384]{2,1,0:T(8,128)(2,1)} %get-tuple-element.39), channel_id=1, source_target_pairs={{0,1},{1,2},{2,3},{3,0},{4,5},{5,6},{6,7},{7,4},{8,9},{9,10},{10,1... | collective-permute-start | bytes 442376 | tf_op jit(solution)/shard_map/ppermute | solution.py:575
  15.7 12.5 %collective-permute-start.1 = (bf16[4,48,384]{2,1,0:T(8,128)(2,1)}, bf16[4,48,384]{2,1,0:T(8,128)(2,1)S(1)}, u32[]{:S(2)}, u32[]{:S(2)}) collective-permute-start(bf16[4,48,384]{2,1,0:T(8,128)(2,1)} %get-tuple-element.40), channel_id=1, source_target_pairs={{0,2},{1,3},{2,0},{3,1},{4,6},{5,7},{6,4},{7,5},{8,10},{9,11},{10,... | collective-permute-start | bytes 442376 | tf_op jit(solution)/shard_map/ppermute | solution.py:575
  18.3 9.9 %collective-permute-start.2 = (bf16[4,48,384]{2,1,0:T(8,128)(2,1)}, bf16[4,48,384]{2,1,0:T(8,128)(2,1)S(1)}, u32[]{:S(2)}, u32[]{:S(2)}) collective-permute-start(bf16[4,48,384]{2,1,0:T(8,128)(2,1)} %get-tuple-element.41), channel_id=1, source_target_pairs={{0,3},{1,0},{2,1},{3,2},{4,7},{5,4},{6,5},{7,6},{8,11},{9,8},{10,9... | collective-permute-start | bytes 442376 | tf_op jit(solution)/shard_map/ppermute | solution.py:575
  19.7 8.6 %copy-start.13 = (bf16[4,48,384]{2,1,0:T(8,128)(2,1)S(1)}, bf16[4,48,384]{2,1,0:T(8,128)(2,1)}, u32[]{:S(2)}) copy-start(bf16[4,48,384]{2,1,0:T(8,128)(2,1)} %get-tuple-element.46) | copy-start | bytes 442372
  26.2 5.7 %copy-start.29 = (bf16[192,768]{1,0:T(8,128)(2,1)S(1)}, bf16[192,768]{1,0:T(8,128)(2,1)}, u32[]{:S(2)}) copy-start(bf16[192,768]{1,0:T(8,128)(2,1)} %get-tuple-element.51) | copy-start | bytes 884740
  26.2 9.3 %copy-start.28 = (bf16[192,768]{1,0:T(8,128)(2,1)S(1)}, bf16[192,768]{1,0:T(8,128)(2,1)}, u32[]{:S(2)}) copy-start(bf16[192,768]{1,0:T(8,128)(2,1)} %get-tuple-element.52) | copy-start | bytes 884740
  26.2 31.4 %copy-start.27 = (bf16[192,768]{1,0:T(8,128)(2,1)S(1)}, bf16[192,768]{1,0:T(8,128)(2,1)}, u32[]{:S(2)}) copy-start(bf16[192,768]{1,0:T(8,128)(2,1)} %get-tuple-element.53) | copy-start | bytes 884740
  28.3 40.4 %copy-start = (bf16[4,4,48,384]{3,2,1,0:T(8,128)(2,1)}, bf16[4,4,48,384]{3,2,1,0:T(8,128)(2,1)S(1)}, u32[]{:S(2)}) copy-start(bf16[4,4,48,384]{3,2,1,0:T(8,128)(2,1)S(1)} %pad_maximum_fusion.rest_0_) | copy-start | bytes 1769476
  28.3 17.2 %collective-permute-start.8 = (bf16[4,4,48,384]{3,2,1,0:T(8,128)(2,1)S(1)}, bf16[4,4,48,384]{3,2,1,0:T(8,128)(2,1)S(1)}, u32[]{:S(2)}, u32[]{:S(2)}) collective-permute-start(bf16[4,4,48,384]{3,2,1,0:T(8,128)(2,1)S(1)} %pad_maximum_fusion.rest_0_), channel_id=1, source_target_pairs={{0,24},{4,28},{8,16},{12,20},{16,8},{20,12},{24,0},{28,4},{1,25},{... | collective-permute-start | bytes 1769480 | tf_op jit(solution)/shard_map/ppermute | solution.py:580
  30.8 26.2 %collective-permute-start.6 = (bf16[4,4,48,384]{3,2,1,0:T(8,128)(2,1)S(1)}, bf16[4,4,48,384]{3,2,1,0:T(8,128)(2,1)S(1)}, u32[]{:S(2)}, u32[]{:S(2)}) collective-permute-start(bf16[4,4,48,384]{3,2,1,0:T(8,128)(2,1)S(1)} %pad_maximum_fusion.rest_0_), channel_id=1, source_target_pairs={{0,16},{4,20},{8,24},{12,28},{16,0},{20,4},{24,8},{28,12},{1,17},{... | collective-permute-start | bytes 1769480 | tf_op jit(solution)/shard_map/ppermute | solution.py:580
  31.3 25.8 %collective-permute-start.4 = (bf16[4,4,48,384]{3,2,1,0:T(8,128)(2,1)S(1)}, bf16[4,4,48,384]{3,2,1,0:T(8,128)(2,1)S(1)}, u32[]{:S(2)}, u32[]{:S(2)}) collective-permute-start(bf16[4,4,48,384]{3,2,1,0:T(8,128)(2,1)S(1)} %pad_maximum_fusion.rest_0_), channel_id=1, source_target_pairs={{0,8},{4,12},{8,0},{12,4},{16,24},{20,28},{24,16},{28,20},{1,9},{5... | collective-permute-start | bytes 1769480 | tf_op jit(solution)/shard_map/ppermute | solution.py:580
  31.9 12.7 %collective-permute-start.10 = (bf16[192,768]{1,0:T(8,128)(2,1)S(1)}, bf16[192,768]{1,0:T(8,128)(2,1)S(1)}, u32[]{:S(2)}, u32[]{:S(2)}) collective-permute-start(bf16[192,768]{1,0:T(8,128)(2,1)S(1)} %copy-done.29), channel_id=1, source_target_pairs={{0,1},{1,2},{2,3},{3,0},{4,5},{5,6},{6,7},{7,4},{8,9},{9,10},{10,1... | collective-permute-start | bytes 884744 | tf_op jit(solution)/shard_map/ppermute | solution.py:575
  35.5 22.1 %collective-permute-start.11 = (bf16[192,768]{1,0:T(8,128)(2,1)S(1)}, bf16[192,768]{1,0:T(8,128)(2,1)S(1)}, u32[]{:S(2)}, u32[]{:S(2)}) collective-permute-start(bf16[192,768]{1,0:T(8,128)(2,1)S(1)} %copy-done.28), channel_id=1, source_target_pairs={{0,2},{1,3},{2,0},{3,1},{4,6},{5,7},{6,4},{7,5},{8,10},{9,11},{10,... | collective-permute-start | bytes 884744 | tf_op jit(solution)/shard_map/ppermute | solution.py:575
  44.6 24.1 %copy-start.8 = (bf16[192,768]{1,0:T(8,128)(2,1)}, bf16[192,768]{1,0:T(8,128)(2,1)S(1)}, u32[]{:S(2)}) copy-start(bf16[192,768]{1,0:T(8,128)(2,1)S(1)} %collective-permute-done.10.rest_9_) | copy-start | bytes 884740
  44.6 24.1 %collective-permute-start.3 = (bf16[4,4,48,384]{3,2,1,0:T(8,128)(2,1)S(1)}, bf16[4,4,48,384]{3,2,1,0:T(8,128)(2,1)S(1)}, u32[]{:S(2)}, u32[]{:S(2)}) collective-permute-start(bf16[4,4,48,384]{3,2,1,0:T(8,128)(2,1)S(1)} %pad_maximum_fusion.rest_0_), channel_id=1, source_target_pairs={{0,4},{4,0},{8,12},{12,8},{16,20},{20,16},{24,28},{28,24},{1,5},{5... | collective-permute-start | bytes 1769480 | tf_op jit(solution)/shard_map/ppermute | solution.py:580
  45.5 23.2 %copy-start.1 = (bf16[4,4,48,384]{3,2,1,0:T(8,128)(2,1)}, bf16[4,4,48,384]{3,2,1,0:T(8,128)(2,1)S(1)}, u32[]{:S(2)}) copy-start(bf16[4,4,48,384]{3,2,1,0:T(8,128)(2,1)S(1)} %collective-permute-done.8.rest_6_) | copy-start | bytes 1769476
  45.5 23.1 %collective-permute-start.9 = (bf16[4,4,48,384]{3,2,1,0:T(8,128)(2,1)S(1)}, bf16[4,4,48,384]{3,2,1,0:T(8,128)(2,1)S(1)}, u32[]{:S(2)}, u32[]{:S(2)}) collective-permute-start(bf16[4,4,48,384]{3,2,1,0:T(8,128)(2,1)S(1)} %collective-permute-done.8.rest_6_), channel_id=1, source_target_pairs={{0,4},{4,0},{8,12},{12,8},{16,20},{20,16},{24,28},{28,24},{1,5},{5... | collective-permute-start | bytes 1769480 | tf_op jit(solution)/shard_map/ppermute | solution.py:580
  57.1 11.7 %copy-start.2 = (bf16[4,4,48,384]{3,2,1,0:T(8,128)(2,1)}, bf16[4,4,48,384]{3,2,1,0:T(8,128)(2,1)S(1)}, u32[]{:S(2)}) copy-start(bf16[4,4,48,384]{3,2,1,0:T(8,128)(2,1)S(1)} %collective-permute-done.6.rest_4_) | copy-start | bytes 1769476
  57.1 11.6 %collective-permute-start.7 = (bf16[4,4,48,384]{3,2,1,0:T(8,128)(2,1)S(1)}, bf16[4,4,48,384]{3,2,1,0:T(8,128)(2,1)S(1)}, u32[]{:S(2)}, u32[]{:S(2)}) collective-permute-start(bf16[4,4,48,384]{3,2,1,0:T(8,128)(2,1)S(1)} %collective-permute-done.6.rest_4_), channel_id=1, source_target_pairs={{0,4},{4,0},{8,12},{12,8},{16,20},{20,16},{24,28},{28,24},{1,5},{5... | collective-permute-start | bytes 1769480 | tf_op jit(solution)/shard_map/ppermute | solution.py:580
  57.2 11.6 %copy-start.3 = (bf16[4,4,48,384]{3,2,1,0:T(8,128)(2,1)}, bf16[4,4,48,384]{3,2,1,0:T(8,128)(2,1)S(1)}, u32[]{:S(2)}) copy-start(bf16[4,4,48,384]{3,2,1,0:T(8,128)(2,1)S(1)} %collective-permute-done.4.rest_2_) | copy-start | bytes 1769476
  57.2 11.5 %collective-permute-start.5 = (bf16[4,4,48,384]{3,2,1,0:T(8,128)(2,1)S(1)}, bf16[4,4,48,384]{3,2,1,0:T(8,128)(2,1)S(1)}, u32[]{:S(2)}, u32[]{:S(2)}) collective-permute-start(bf16[4,4,48,384]{3,2,1,0:T(8,128)(2,1)S(1)} %collective-permute-done.4.rest_2_), channel_id=1, source_target_pairs={{0,4},{4,0},{8,12},{12,8},{16,20},{20,16},{24,28},{28,24},{1,5},{5... | collective-permute-start | bytes 1769480 | tf_op jit(solution)/shard_map/ppermute | solution.py:580
  57.6 11.1 %copy-start.9 = (bf16[192,768]{1,0:T(8,128)(2,1)}, bf16[192,768]{1,0:T(8,128)(2,1)S(1)}, u32[]{:S(2)}) copy-start(bf16[192,768]{1,0:T(8,128)(2,1)S(1)} %collective-permute-done.11.rest_10_) | copy-start | bytes 884740
  57.6 11.0 %collective-permute-start.12 = (bf16[192,768]{1,0:T(8,128)(2,1)S(1)}, bf16[192,768]{1,0:T(8,128)(2,1)S(1)}, u32[]{:S(2)}, u32[]{:S(2)}) collective-permute-start(bf16[192,768]{1,0:T(8,128)(2,1)S(1)} %copy-done.27), channel_id=1, source_target_pairs={{0,3},{1,0},{2,1},{3,2},{4,7},{5,4},{6,5},{7,6},{8,11},{9,8},{10,9... | collective-permute-start | bytes 884744 | tf_op jit(solution)/shard_map/ppermute | solution.py:575
  68.7 0.7 copy-start.10
  68.7 0.9 copy-start.4
  68.7 1.1 copy-start.5
  68.7 1.3 copy-start.6
  70.0 0.8 copy-start.7
  80.6 51.1 %collective-permute-start.29 = (bf16[4,4,2,48,384]{4,3,2,1,0:T(8,128)(2,1)}, bf16[4,4,2,48,384]{4,3,2,1,0:T(8,128)(2,1)S(1)}, u32[]{:S(2)}, u32[]{:S(2)}) collective-permute-start(bf16[4,4,2,48,384]{4,3,2,1,0:T(8,128)(2,1)} %get-tuple-element.68), channel_id=1, source_target_pairs={{0,4},{4,0},{8,12},{12,8},{16,20},{20,16},{24,28},{28,24},{1,5},{5... | collective-permute-start | bytes 3538952 | tf_op jit(solution)/shard_map/ppermute | solution.py:580
  80.7 17.4 %collective-permute-start.16 = (bf16[192,384]{1,0:T(8,128)(2,1)}, bf16[192,384]{1,0:T(8,128)(2,1)S(1)}, u32[]{:S(2)}, u32[]{:S(2)}) collective-permute-start(bf16[192,384]{1,0:T(8,128)(2,1)} %get-tuple-element.59), channel_id=1, source_target_pairs={{0,3},{1,0},{2,1},{3,2},{4,7},{5,4},{6,5},{7,6},{8,11},{9,8},{10,9... | collective-permute-start | bytes 442376 | tf_op jit(solution)/shard_map/ppermute | solution.py:575
  84.3 15.0 %collective-permute-start.17 = (bf16[192,384]{1,0:T(8,128)(2,1)}, bf16[192,384]{1,0:T(8,128)(2,1)S(1)}, u32[]{:S(2)}, u32[]{:S(2)}) collective-permute-start(bf16[192,384]{1,0:T(8,128)(2,1)} %get-tuple-element.60), channel_id=1, source_target_pairs={{0,2},{1,3},{2,0},{3,1},{4,6},{5,7},{6,4},{7,5},{8,10},{9,11},{10,... | collective-permute-start | bytes 442376 | tf_op jit(solution)/shard_map/ppermute | solution.py:575
  84.3 15.0 %collective-permute-start.18 = (bf16[192,384]{1,0:T(8,128)(2,1)}, bf16[192,384]{1,0:T(8,128)(2,1)S(1)}, u32[]{:S(2)}, u32[]{:S(2)}) collective-permute-start(bf16[192,384]{1,0:T(8,128)(2,1)} %get-tuple-element.61), channel_id=1, source_target_pairs={{0,1},{1,2},{2,3},{3,0},{4,5},{5,6},{6,7},{7,4},{8,9},{9,10},{10,1... | collective-permute-start | bytes 442376 | tf_op jit(solution)/shard_map/ppermute | solution.py:575
  94.7 8.0 %collective-permute-start.13 = (bf16[192,384]{1,0:T(8,128)(2,1)}, bf16[192,384]{1,0:T(8,128)(2,1)S(1)}, u32[]{:S(2)}, u32[]{:S(2)}) collective-permute-start(bf16[192,384]{1,0:T(8,128)(2,1)} %get-tuple-element.55), channel_id=1, source_target_pairs={{0,3},{1,0},{2,1},{3,2},{4,7},{5,4},{6,5},{7,6},{8,11},{9,8},{10,9... | collective-permute-start | bytes 442376 | tf_op jit(solution)/shard_map/ppermute | solution.py:575
  98.1 14.2 %copy-start.14 = (bf16[192,384]{1,0:T(8,128)(2,1)}, bf16[192,384]{1,0:T(8,128)(2,1)S(1)}, u32[]{:S(2)}) copy-start(bf16[192,384]{1,0:T(8,128)(2,1)S(1)} %collective-permute-done.16.rest_5_) | copy-start | bytes 442372
  98.1 14.1 %collective-permute-start.14 = (bf16[192,384]{1,0:T(8,128)(2,1)}, bf16[192,384]{1,0:T(8,128)(2,1)S(1)}, u32[]{:S(2)}, u32[]{:S(2)}) collective-permute-start(bf16[192,384]{1,0:T(8,128)(2,1)} %get-tuple-element.56), channel_id=1, source_target_pairs={{0,2},{1,3},{2,0},{3,1},{4,6},{5,7},{6,4},{7,5},{8,10},{9,11},{10,... | collective-permute-start | bytes 442376 | tf_op jit(solution)/shard_map/ppermute | solution.py:575
  99.3 13.0 %copy-start.15 = (bf16[192,384]{1,0:T(8,128)(2,1)}, bf16[192,384]{1,0:T(8,128)(2,1)S(1)}, u32[]{:S(2)}) copy-start(bf16[192,384]{1,0:T(8,128)(2,1)S(1)} %collective-permute-done.17.rest_6_) | copy-start | bytes 442372
  99.3 13.0 %collective-permute-start.15 = (bf16[192,384]{1,0:T(8,128)(2,1)}, bf16[192,384]{1,0:T(8,128)(2,1)S(1)}, u32[]{:S(2)}, u32[]{:S(2)}) collective-permute-start(bf16[192,384]{1,0:T(8,128)(2,1)} %get-tuple-element.57), channel_id=1, source_target_pairs={{0,1},{1,2},{2,3},{3,0},{4,5},{5,6},{6,7},{7,4},{8,9},{9,10},{10,1... | collective-permute-start | bytes 442376 | tf_op jit(solution)/shard_map/ppermute | solution.py:575
  99.3 13.0 %copy-start.16 = (bf16[192,384]{1,0:T(8,128)(2,1)}, bf16[192,384]{1,0:T(8,128)(2,1)S(1)}, u32[]{:S(2)}) copy-start(bf16[192,384]{1,0:T(8,128)(2,1)S(1)} %collective-permute-done.18.rest_7_) | copy-start | bytes 442372
  102.7 9.6 %copy-start.17 = (bf16[192,384]{1,0:T(8,128)(2,1)}, bf16[192,384]{1,0:T(8,128)(2,1)S(1)}, u32[]{:S(2)}) copy-start(bf16[192,384]{1,0:T(8,128)(2,1)S(1)} %collective-permute-done.13.rest_1_) | copy-start | bytes 442372
  112.3 0.7 copy-start.18
  112.3 0.7 copy-start.19
  113.0 8.8 %copy-start.26 = (bf16[4,4,2,48,384]{4,3,2,1,0:T(8,128)(2,1)S(1)}, bf16[4,4,2,48,384]{4,3,2,1,0:T(8,128)(2,1)}, u32[]{:S(2)}) copy-start(bf16[4,4,2,48,384]{4,3,2,1,0:T(8,128)(2,1)} %get-tuple-element.66) | copy-start | bytes 3538948
  120.7 11.1 %copy-start.12 = (bf16[4,4,2,48,384]{4,3,2,1,0:T(8,128)(2,1)S(1)}, bf16[4,4,2,48,384]{4,3,2,1,0:T(8,128)(2,1)}, u32[]{:S(2)}) copy-start(bf16[4,4,2,48,384]{4,3,2,1,0:T(8,128)(2,1)} %get-tuple-element.67) | copy-start | bytes 3538948
  121.7 1.4 collective-permute-start.19
  121.8 14.0 %collective-permute-start.22 = (bf16[4,4,2,48,384]{4,3,2,1,0:T(8,128)(2,1)S(1)}, bf16[4,4,2,48,384]{4,3,2,1,0:T(8,128)(2,1)S(1)}, u32[]{:S(2)}, u32[]{:S(2)}) collective-permute-start(bf16[4,4,2,48,384]{4,3,2,1,0:T(8,128)(2,1)S(1)} %copy-done.26), channel_id=1, source_target_pairs={{0,4},{4,0},{8,12},{12,8},{16,20},{20,16},{24,28},{28,24},{1,5},{5... | collective-permute-start | bytes 3538952 | tf_op jit(solution)/shard_map/ppermute | solution.py:580
  124.2 6.0 %collective-permute-start.20 = (bf16[192,384]{1,0:T(8,128)(2,1)S(1)}, bf16[192,384]{1,0:T(8,128)(2,1)S(1)}, u32[]{:S(2)}, u32[]{:S(2)}) collective-permute-start(bf16[192,384]{1,0:T(8,128)(2,1)S(1)} %add_convert_fusion.1), channel_id=1, source_target_pairs={{0,8},{4,12},{8,0},{12,4},{16,24},{20,28},{24,16},{28,20},{1,9},{5... | collective-permute-start | bytes 442376 | tf_op jit(solution)/shard_map/ppermute | solution.py:580
  130.2 32.0 %collective-permute-start.21 = (bf16[192,384]{1,0:T(8,128)(2,1)S(1)}, bf16[192,384]{1,0:T(8,128)(2,1)S(1)}, u32[]{:S(2)}, u32[]{:S(2)}) collective-permute-start(bf16[192,384]{1,0:T(8,128)(2,1)S(1)} %add_convert_fusion), channel_id=1, source_target_pairs={{0,16},{4,20},{8,24},{12,28},{16,0},{20,4},{24,8},{28,12},{1,17},{... | collective-permute-start | bytes 442376 | tf_op jit(solution)/shard_map/ppermute | solution.py:580
  132.2 3.7 %copy-start.11 = (bf16[4,4,2,48,384]{4,3,2,1,0:T(8,128)(2,1)S(1)}, bf16[4,4,2,48,384]{4,3,2,1,0:T(8,128)(2,1)}, u32[]{:S(2)}) copy-start(bf16[4,4,2,48,384]{4,3,2,1,0:T(8,128)(2,1)} %get-tuple-element.65) | copy-start | bytes 3538948
  132.3 10.0 %collective-permute-start.30 = (bf16[4,2,48,384]{3,2,1,0:T(8,128)(2,1)S(1)}, bf16[4,2,48,384]{3,2,1,0:T(8,128)(2,1)S(1)}, u32[]{:S(2)}, u32[]{:S(2)}) collective-permute-start(bf16[4,2,48,384]{3,2,1,0:T(8,128)(2,1)S(1)} %get-tuple-element.73), channel_id=1, source_target_pairs={{0,8},{4,12},{8,0},{12,4},{16,24},{20,28},{24,16},{28,20},{1,9},{5... | collective-permute-start | bytes 884744 | tf_op jit(solution)/shard_map/ppermute | solution.py:580
  133.1 15.5 %collective-permute-start.32 = (bf16[4,2,48,384]{3,2,1,0:T(8,128)(2,1)S(1)}, bf16[4,2,48,384]{3,2,1,0:T(8,128)(2,1)S(1)}, u32[]{:S(2)}, u32[]{:S(2)}) collective-permute-start(bf16[4,2,48,384]{3,2,1,0:T(8,128)(2,1)S(1)} %get-tuple-element.74), channel_id=1, source_target_pairs={{0,24},{4,28},{8,16},{12,20},{16,8},{20,12},{24,0},{28,4},{1,25},{... | collective-permute-start | bytes 884744 | tf_op jit(solution)/shard_map/ppermute | solution.py:580
  134.3 15.8 %collective-permute-start.31 = (bf16[4,2,48,384]{3,2,1,0:T(8,128)(2,1)S(1)}, bf16[4,2,48,384]{3,2,1,0:T(8,128)(2,1)S(1)}, u32[]{:S(2)}, u32[]{:S(2)}) collective-permute-start(bf16[4,2,48,384]{3,2,1,0:T(8,128)(2,1)S(1)} %get-tuple-element.75), channel_id=1, source_target_pairs={{0,16},{4,20},{8,24},{12,28},{16,0},{20,4},{24,8},{28,12},{1,17},{... | collective-permute-start | bytes 884744 | tf_op jit(solution)/shard_map/ppermute | solution.py:580
  136.3 18.6 %collective-permute-start.23 = (bf16[4,2,48,384]{3,2,1,0:T(8,128)(2,1)S(1)}, bf16[4,2,48,384]{3,2,1,0:T(8,128)(2,1)S(1)}, u32[]{:S(2)}, u32[]{:S(2)}) collective-permute-start(bf16[4,2,48,384]{3,2,1,0:T(8,128)(2,1)S(1)} %get-tuple-element.76), channel_id=1, source_target_pairs={{0,8},{4,12},{8,0},{12,4},{16,24},{20,28},{24,16},{28,20},{1,9},{5... | collective-permute-start | bytes 884744 | tf_op jit(solution)/shard_map/ppermute | solution.py:580
  142.3 17.1 %collective-permute-start.25 = (bf16[4,2,48,384]{3,2,1,0:T(8,128)(2,1)S(1)}, bf16[4,2,48,384]{3,2,1,0:T(8,128)(2,1)S(1)}, u32[]{:S(2)}, u32[]{:S(2)}) collective-permute-start(bf16[4,2,48,384]{3,2,1,0:T(8,128)(2,1)S(1)} %get-tuple-element.77), channel_id=1, source_target_pairs={{0,24},{4,28},{8,16},{12,20},{16,8},{20,12},{24,0},{28,4},{1,25},{... | collective-permute-start | bytes 884744 | tf_op jit(solution)/shard_map/ppermute | solution.py:580
  148.6 12.4 %collective-permute-start.24 = (bf16[4,2,48,384]{3,2,1,0:T(8,128)(2,1)S(1)}, bf16[4,2,48,384]{3,2,1,0:T(8,128)(2,1)S(1)}, u32[]{:S(2)}, u32[]{:S(2)}) collective-permute-start(bf16[4,2,48,384]{3,2,1,0:T(8,128)(2,1)S(1)} %get-tuple-element.78), channel_id=1, source_target_pairs={{0,16},{4,20},{8,24},{12,28},{16,0},{20,4},{24,8},{28,12},{1,17},{... | collective-permute-start | bytes 884744 | tf_op jit(solution)/shard_map/ppermute | solution.py:580
  150.9 12.7 %collective-permute-start.35 = (bf16[2,48,384]{2,1,0:T(8,128)(2,1)S(1)}, bf16[2,48,384]{2,1,0:T(8,128)(2,1)S(1)}, u32[]{:S(2)}, u32[]{:S(2)}) collective-permute-start(bf16[2,48,384]{2,1,0:T(8,128)(2,1)S(1)} %get-tuple-element.79), channel_id=1, source_target_pairs={{0,1},{1,2},{2,3},{3,0},{4,5},{5,6},{6,7},{7,4},{8,9},{9,10},{10,1... | collective-permute-start | bytes 221192 | tf_op jit(solution)/shard_map/ppermute | solution.py:575
  155.0 12.0 %collective-permute-start.34 = (bf16[2,48,384]{2,1,0:T(8,128)(2,1)S(1)}, bf16[2,48,384]{2,1,0:T(8,128)(2,1)S(1)}, u32[]{:S(2)}, u32[]{:S(2)}) collective-permute-start(bf16[2,48,384]{2,1,0:T(8,128)(2,1)S(1)} %get-tuple-element.80), channel_id=1, source_target_pairs={{0,2},{1,3},{2,0},{3,1},{4,6},{5,7},{6,4},{7,5},{8,10},{9,11},{10,... | collective-permute-start | bytes 221192 | tf_op jit(solution)/shard_map/ppermute | solution.py:575
  159.4 7.6 %collective-permute-start.33 = (bf16[2,48,384]{2,1,0:T(8,128)(2,1)S(1)}, bf16[2,48,384]{2,1,0:T(8,128)(2,1)S(1)}, u32[]{:S(2)}, u32[]{:S(2)}) collective-permute-start(bf16[2,48,384]{2,1,0:T(8,128)(2,1)S(1)} %get-tuple-element.81), channel_id=1, source_target_pairs={{0,3},{1,0},{2,1},{3,2},{4,7},{5,4},{6,5},{7,6},{8,11},{9,8},{10,9... | collective-permute-start | bytes 221192 | tf_op jit(solution)/shard_map/ppermute | solution.py:575
  161.8 6.3 %collective-permute-start.28 = (bf16[2,48,384]{2,1,0:T(8,128)(2,1)S(1)}, bf16[2,48,384]{2,1,0:T(8,128)(2,1)S(1)}, u32[]{:S(2)}, u32[]{:S(2)}) collective-permute-start(bf16[2,48,384]{2,1,0:T(8,128)(2,1)S(1)} %get-tuple-element.83), channel_id=1, source_target_pairs={{0,1},{1,2},{2,3},{3,0},{4,5},{5,6},{6,7},{7,4},{8,9},{9,10},{10,1... | collective-permute-start | bytes 221192 | tf_op jit(solution)/shard_map/ppermute | solution.py:575
  162.2 6.8 %collective-permute-start.27 = (bf16[2,48,384]{2,1,0:T(8,128)(2,1)S(1)}, bf16[2,48,384]{2,1,0:T(8,128)(2,1)S(1)}, u32[]{:S(2)}, u32[]{:S(2)}) collective-permute-start(bf16[2,48,384]{2,1,0:T(8,128)(2,1)S(1)} %get-tuple-element.84), channel_id=1, source_target_pairs={{0,2},{1,3},{2,0},{3,1},{4,6},{5,7},{6,4},{7,5},{8,10},{9,11},{10,... | collective-permute-start | bytes 221192 | tf_op jit(solution)/shard_map/ppermute | solution.py:575
  163.6 5.4 %copy-start.20 = (bf16[2,48,384]{2,1,0:T(8,128)(2,1)}, bf16[2,48,384]{2,1,0:T(8,128)(2,1)S(1)}, u32[]{:S(2)}) copy-start(bf16[2,48,384]{2,1,0:T(8,128)(2,1)S(1)} %collective-permute-done.35.rest_7_) | copy-start | bytes 221188
  163.6 5.4 %collective-permute-start.26 = (bf16[2,48,384]{2,1,0:T(8,128)(2,1)S(1)}, bf16[2,48,384]{2,1,0:T(8,128)(2,1)S(1)}, u32[]{:S(2)}, u32[]{:S(2)}) collective-permute-start(bf16[2,48,384]{2,1,0:T(8,128)(2,1)S(1)} %get-tuple-element.85), channel_id=1, source_target_pairs={{0,3},{1,0},{2,1},{3,2},{4,7},{5,4},{6,5},{7,6},{8,11},{9,8},{10,9... | collective-permute-start | bytes 221192 | tf_op jit(solution)/shard_map/ppermute | solution.py:575
  166.9 2.1 %copy-start.21 = (bf16[2,48,384]{2,1,0:T(8,128)(2,1)}, bf16[2,48,384]{2,1,0:T(8,128)(2,1)S(1)}, u32[]{:S(2)}) copy-start(bf16[2,48,384]{2,1,0:T(8,128)(2,1)S(1)} %collective-permute-done.34.rest_6_) | copy-start | bytes 221188
  167.0 2.1 %copy-start.22 = (bf16[2,48,384]{2,1,0:T(8,128)(2,1)}, bf16[2,48,384]{2,1,0:T(8,128)(2,1)S(1)}, u32[]{:S(2)}) copy-start(bf16[2,48,384]{2,1,0:T(8,128)(2,1)S(1)} %collective-permute-done.33.rest_5_) | copy-start | bytes 221188
  168.1 0.9 copy-start.23
  (2 other events, 1.3 us)
